TPU v7x, 32 devices: a whole 2x2x4 slice. The times are simulated.
32 devices in a mesh: seq: 8 (over z, y), exp: 4 (over x, core).
Axes of the slice: x: 2, y: 2, z: 4, core: 2. Of those that a mesh axis runs over, the one named last changes fastest.
Arguments:
- residual_in: bfloat16 [4096, 2048], P(('seq', 'exp')), may hold values from -6 to 6
- query_input: bfloat16 [4096, 1024], P(('seq', 'exp')), may hold values from -6 to 6
- key_input: bfloat16 [4096, 1024], P(('seq', 'exp')), may hold values from -6 to 6
- value_input: bfloat16 [4096, 2048], P(('seq', 'exp')), may hold values from -6 to 6
- out_gate: bfloat16 [4096, 2048], P(('seq', 'exp')), may hold values from -6 to 6
- write_strength: float32 [4096, 16], P(('seq', 'exp')), may hold values from 0 to 2
- decay_rate: float32 [4096, 16], P(('seq', 'exp')), may hold values from 0 to 1
- head_gain: float32 [128], replicated, may hold values from 0.1 to 1.9
- out_proj: bfloat16 [2048, 2048], P(None, 'exp'), may hold values from -0.125 to 0.125
- post_gain: float32 [2048], replicated, may hold values from 0.1 to 1.9
- expert_ids: int32 [4096, 10], P(('seq', 'exp')), may hold values from 0 to 63, all different within a row; in each aligned block of 128 rows (0 to 127, 128 to 255, ...) at most 32 rows name the same one
- gate_weights: float32 [4096, 10], P(('seq', 'exp')), may hold values from 0.05 to 0.3
- expert_gate: bfloat16 [64, 2048, 512], P(('seq', 'exp')), may hold values from -0.125 to 0.125
- expert_up: bfloat16 [64, 2048, 512], P(('seq', 'exp')), may hold values from -0.125 to 0.125
- expert_down: bfloat16 [64, 512, 2048], P(('seq', 'exp')), may hold values from -0.25 to 0.25
Outputs:
- layer_out: bfloat16 [4096, 2048], P(('seq', 'exp'))
Inputs may be any that keep to these rules, and one draw needn't show every extreme that they name: `expert_ids`: each row names 10 different experts. Within the rows of one device (aligned blocks of 128 rows) no expert is named more than 32 times, and in every draw some expert is named exactly 32 times within one device's rows.
All inputs are finite; a program needn't handle non-finite values.
Results may differ from a plain program's by a relative error of at most 0.011.
Values may be sent and summed in bfloat16 or wider, within the bound.
No kernel may reach another device: no remote copies, remote signals or barrier semaphores. Data moves between devices by JAX's collectives and lax.ppermute only.
A program may use at most 256 MiB of HBM per device.

v0:
```python
import functools

import jax
import jax.numpy as jnp
from jax import lax
from jax.experimental import pallas as pl
from jax.experimental.pallas import tpu as pltpu
from jax.sharding import Mesh, PartitionSpec as P

D = 2048
HK = 8
GROUP_VALUE_HEADS = 16
DK = 128
DV = 128
TOP = 10
HEADS_STEP = 4
BLOCKS_STEP = 16
GROUPS = (1536, 512)
STRIP = 256
EARLY_ROWS = 896

F32 = jnp.float32
BF16 = jnp.bfloat16
AXES = ("outer", "mid", "core", "inner")
SAME_CORE = ("outer", "mid", "inner")
REST = ("mid", "inner")
MIB = 1 << 20


def halves(x):
    high = x.astype(BF16)
    return high, (x - high.astype(F32)).astype(BF16)


def dot(a, b):
    return jnp.dot(a, b, preferred_element_type=F32)


def product(left, right):
    n = right[0].shape[1]
    lhs = jnp.concatenate(left, axis=1)
    top = jnp.concatenate(right, axis=1)
    bottom = jnp.concatenate([right[0], jnp.zeros_like(right[0])], axis=1)
    both = dot(lhs, jnp.concatenate([top, bottom], axis=0))
    return both[:, :n] + both[:, n:]


def local_kernel(q_ref, k_ref, v_ref, logs_ref, logs_row_ref, strength_row_ref, strength_ref, maps_ref, mix_ref):
    n = k_ref.shape[0]
    row = lax.broadcasted_iota(jnp.int32, (n, n), 0)
    column = lax.broadcasted_iota(jnp.int32, (n, n), 1)
    inclusive, strict, diagonal = row >= column, row > column, row == column
    heads = maps_ref.shape[0]
    group = GROUP_VALUE_HEADS // HK
    identity = diagonal.astype(F32)

    keys = []
    for i in range(heads // group):
        lanes = slice(i * DK, (i + 1) * DK)
        k_raw, q_raw = k_ref[:, lanes], q_ref[:, lanes]
        k_wide, q_wide = k_raw.astype(F32), q_raw.astype(F32)
        dims = (((1,), (1,)), ((), ()))
        gram = lax.dot_general(k_raw, k_raw, dims, preferred_element_type=F32)
        scores = lax.dot_general(q_raw, k_raw, dims, preferred_element_type=F32)
        inv_k = lax.rsqrt(jnp.sum(k_wide * k_wide, axis=1, keepdims=True) + 1e-06)
        inv_k_row = lax.rsqrt(jnp.sum(jnp.where(diagonal, gram, 0.0), axis=0, keepdims=True) + 1e-06)
        inv_q = lax.rsqrt(jnp.sum(q_wide * q_wide, axis=1, keepdims=True) + 1e-06) * DK ** (-0.5)
        keys.append(
            dict(
                k=k_raw,
                k_t=jnp.transpose(k_wide).astype(BF16),
                q=q_wide * inv_q,
                gram=gram * inv_k * inv_k_row,
                scores=scores * inv_q * inv_k_row,
                inv=inv_k,
                inv_row=inv_k_row,
            )
        )

    ratios, systems, inverses = [], [], []
    for j in range(heads):
        logs, logs_row = logs_ref[0][:, j : j + 1], logs_row_ref[0][j : j + 1, :]
        ratio = jnp.where(inclusive, jnp.exp(jnp.where(inclusive, logs - logs_row, 0.0)), 0.0)
        system = jnp.where(strict, ratio * keys[j // group]["gram"], 0.0) * strength_ref[0][:, j : j + 1]
        first = (row // 2 == column // 2) & strict
        ratios.append(ratio)
        systems.append(halves(system))
        inverses.append(identity - jnp.where(first, system, 0.0))
    size = 2
    while size < n:
        pairs = (row // (2 * size) == column // (2 * size)) & (row // size > column // size)
        inverse_halves = [halves(t) for t in inverses]
        cut = [
            tuple(jnp.where(pairs, part.astype(F32), 0.0).astype(BF16) for part in s) for s in systems
        ]
        left = [product(t, c) for t, c in zip(inverse_halves, cut)]
        inverses = [
            t - product(halves(x), th) for t, x, th in zip(inverses, left, inverse_halves)
        ]
        size *= 2

    for j in range(heads):
        key = keys[j // group]
        logs, logs_row = logs_ref[0][:, j : j + 1], logs_row_ref[0][j : j + 1, :]
        strength_row = strength_row_ref[0][j : j + 1, :]
        value = v_ref[:, j * DV : (j + 1) * DV]
        t = inverses[j]
        new_value = dot(
            jnp.concatenate(halves(t * strength_row), axis=1), jnp.concatenate([value, value], axis=0)
        )
        key_matrix = dot(
            jnp.concatenate(halves(t * (strength_row * jnp.exp(logs_row) * key["inv_row"])), axis=1),
            jnp.concatenate([key["k"], key["k"]], axis=0),
        )
        both = jnp.concatenate([key_matrix, new_value], axis=1)
        last = logs[n - 1 : n, :]
        faded = halves(both * (jnp.exp(last - logs) * key["inv"]))
        state = dot(
            jnp.concatenate([key["k_t"], key["k_t"]], axis=1), jnp.concatenate(faded, axis=0)
        )
        high, low = halves(jnp.exp(last) * identity - state[:, :DK])
        maps_ref[j, :, :DK] = high
        maps_ref[j, :, DK : 2 * DK] = low
        maps_ref[j, :, 2 * DK :] = state[:, DK:].astype(BF16)
        mixed = halves(ratios[j] * key["scores"])
        both_halves = halves(both)
        out = dot(
            jnp.concatenate(mixed, axis=1), jnp.concatenate([both_halves[0], both_halves[0]], axis=0)
        ) + dot(mixed[0], both_halves[1])
        mix_ref[j, :, :DK] = key["q"] * jnp.exp(logs) - out[:, :DK]
        mix_ref[j, :, DK:] = out[:, DK:]


def local_terms(query_input, key_input, value_input, write_strength, decay_rate):
    n = key_input.shape[0]
    groups, per_key = GROUP_VALUE_HEADS // HEADS_STEP, GROUP_VALUE_HEADS // HK
    lower = jnp.tril(jnp.ones((n, n), F32))
    logs = jnp.dot(lower, -decay_rate, precision=lax.Precision.HIGHEST)

    def columns(x):
        return jnp.swapaxes(x.reshape(n, groups, HEADS_STEP), 0, 1)

    def rows(x):
        return x.T.reshape(groups, HEADS_STEP, n)

    wide = HEADS_STEP // per_key * DK
    column_spec = pl.BlockSpec((1, n, HEADS_STEP), lambda i: (i, 0, 0))
    row_spec = pl.BlockSpec((1, HEADS_STEP, n), lambda i: (i, 0, 0))
    out_spec = pl.BlockSpec((HEADS_STEP, DK, 2 * DK + DV), lambda i: (i, 0, 0))
    mix_spec = pl.BlockSpec((HEADS_STEP, n, DK + DV), lambda i: (i, 0, 0))
    return pl.pallas_call(
        local_kernel,
        grid=(groups,),
        in_specs=[
            pl.BlockSpec((n, wide), lambda i: (0, i)),
            pl.BlockSpec((n, wide), lambda i: (0, i)),
            pl.BlockSpec((n, HEADS_STEP * DV), lambda i: (0, i)),
            column_spec,
            row_spec,
            row_spec,
            column_spec,
        ],
        out_specs=[out_spec, mix_spec],
        out_shape=[
            jax.ShapeDtypeStruct((GROUP_VALUE_HEADS, DK, 2 * DK + DV), BF16),
            jax.ShapeDtypeStruct((GROUP_VALUE_HEADS, n, DK + DV), F32),
        ],
        compiler_params=pltpu.CompilerParams(vmem_limit_bytes=40 * MIB),
        name="local_terms",
    )(
        query_input,
        key_input,
        value_input,
        columns(logs),
        rows(logs),
        rows(write_strength),
        columns(write_strength),
    )


def chain_kernel(maps_ref, *refs):
    *_, before_ref, whole_ref = refs
    row = lax.broadcasted_iota(jnp.int32, (DK, DK + DV), 0)
    column = lax.broadcasted_iota(jnp.int32, (DK, DK + DV), 1)
    passed = (row == column).astype(F32)
    for i in range(maps_ref.shape[0]):
        before_ref[i] = passed
        high, low = halves(passed)
        passed = dot(maps_ref[i, :, : 2 * DK], jnp.concatenate([high, high], axis=0)) + dot(
            maps_ref[i, :, :DK], low
        )
        passed = jnp.concatenate(
            [passed[:, :DK], passed[:, DK:] + maps_ref[i, :, 2 * DK :].astype(F32)], axis=1
        )
    whole_ref[...] = passed


def chain(maps, *others):
    count = maps.shape[0]
    return pl.pallas_call(
        chain_kernel,
        in_specs=[pl.BlockSpec(memory_space=pltpu.VMEM)]
        + [pl.BlockSpec(memory_space=pl.ANY)] * len(others),
        out_shape=[
            jax.ShapeDtypeStruct((count, DK, DK + DV), F32),
            jax.ShapeDtypeStruct((DK, DK + DV), F32),
        ],
        compiler_params=pltpu.CompilerParams(vmem_limit_bytes=40 * MIB),
        name="chain",
    )(maps, *others)


def tie_kernel(*refs):
    pass


def after(array, *others):
    anywhere = pl.BlockSpec(memory_space=pl.ANY)
    return pl.pallas_call(
        tie_kernel,
        in_specs=[anywhere] * (1 + len(others)),
        out_specs=anywhere,
        out_shape=jax.ShapeDtypeStruct(array.shape, array.dtype),
        input_output_aliases={0: 0},
        name="after",
    )(array, *others)


def entering_states(maps, devices, others, late):
    heads = maps.shape[0]
    segments = devices // heads
    groups = [[g * heads + h for h in range(heads)] for g in range(segments)]
    by_device = lax.all_to_all(
        maps, AXES, split_axis=0, concat_axis=0, axis_index_groups=groups, tiled=True
    )
    before, whole = chain(by_device, *others)
    if segments == 2:
        start = lax.ppermute(whole[:, DK:], AXES, [(h, heads + h) for h in range(heads)])
    else:
        across = [[g * heads + h for g in range(segments)] for h in range(heads)]
        adds = lax.all_gather(whole[:, DK:], AXES, axis_index_groups=across)
        steps = lax.all_gather(whole[:, :DK], AXES, axis_index_groups=across)
        segment = lax.axis_index(AXES) // heads
        carry = adds[0]
        start = jnp.where(segment == 1, carry, 0.0)
        for g in range(2, segments):
            carry = adds[g - 1] + jnp.dot(steps[g - 1], carry, precision=lax.Precision.HIGHEST)
            start = jnp.where(segment == g, carry, start)
    start = after(start, *late)
    states = (
        jnp.dot(
            before[:, :, :DK].reshape(heads * DK, DK), start, precision=lax.Precision.HIGH
        ).reshape(heads, DK, DV)
        + before[:, :, DK:]
    ).astype(BF16)
    back = lax.all_to_all(
        states, AXES, split_axis=0, concat_axis=0, axis_index_groups=groups, tiled=True
    )
    return back


def finish_kernel(
    parts, place_ref, mix_ref, state_ref, gate_ref, gain_ref, residual_ref, post_ref, *refs
):
    *proj_refs, hidden_ref, first_ref, second_ref, core_ref = refs
    for h in range(GROUP_VALUE_HEADS):
        lanes = slice(h * DV, (h + 1) * DV)
        state = state_ref[h]
        recurrent = (
            dot(
                jnp.concatenate(halves(mix_ref[h, :, :DK]), axis=1),
                jnp.concatenate([state, state], axis=0),
            )
            + mix_ref[h, :, DK:]
        )
        inv_rms = lax.rsqrt(jnp.mean(recurrent * recurrent, axis=1, keepdims=True) + 1e-06)
        gate = gate_ref[:, lanes].astype(F32)
        act = gate / (1.0 + jnp.exp(-gate))
        core_ref[:, lanes] = (recurrent * inv_rms * gain_ref[...] * act).astype(BF16)
    core = core_ref[...]
    squares = 0.0
    proj_refs = list(proj_refs)
    for i, count in enumerate(parts):
        refs, proj_refs = proj_refs[:count], proj_refs[count:]
        wide = refs[0].shape[1]
        lanes = pl.ds(pl.multiple_of(place_ref[i] * wide, wide), wide)
        mixed, first = residual_ref[:, lanes].astype(F32), 0
        for ref in refs:
            mixed += dot(core[:, first : first + ref.shape[0]], ref[...])
            first += ref.shape[0]
        hidden = mixed.astype(BF16)
        hidden_ref[:, lanes] = hidden
        widened = hidden.astype(F32)
        squares += jnp.sum(widened * widened, axis=1, keepdims=True)
    inv_rms = lax.rsqrt(squares * (1.0 / D) + 1e-06)
    normed = (hidden_ref[...].astype(F32) * inv_rms * post_ref[...]).astype(BF16)
    start = 0
    for ref, width in zip((first_ref, second_ref), GROUPS):
        ref[...] = normed[:, start : start + width]
        start += width


def finish(mix, states, out_gate, head_gain, proj, places, residual_in, post_gain):
    shape = residual_in.shape
    vmem = pl.BlockSpec(memory_space=pltpu.VMEM)
    flat = [part for piece in proj for part in piece]
    return pl.pallas_call(
        functools.partial(finish_kernel, [len(piece) for piece in proj]),
        in_specs=[pl.BlockSpec(memory_space=pltpu.SMEM)] + [vmem] * (6 + len(flat)),
        out_shape=[
            jax.ShapeDtypeStruct((shape[0], wide), BF16) for wide in (D,) + GROUPS
        ],
        scratch_shapes=[pltpu.VMEM(shape, BF16)],
        compiler_params=pltpu.CompilerParams(vmem_limit_bytes=48 * MIB),
        name="finish",
    )(
        places,
        mix,
        states,
        out_gate,
        head_gain.reshape(1, DV),
        residual_in,
        post_gain.reshape(1, D),
        *flat,
    )


def hidden_units_kernel(
    capacity,
    pieces,
    slot_row_ref,
    slot_ref,
    weight_ref,
    own_gate_ref,
    own_up_ref,
    other_gate_ref,
    other_up_ref,
    *refs,
):
    *token_refs, inner_ref, spread_ref, block_ref, taken_ref, sems = refs
    group, expert = pl.program_id(0), pl.program_id(1)
    blocks, rows, _ = block_ref.shape
    served = taken_ref.shape[0]
    joined = max(1, 16 // capacity)

    def copies(step, b):
        found = []
        start = 0
        for part, width in enumerate(GROUPS):
            for ref, (column, places) in zip(token_refs, pieces):
                place = step * blocks + b
                if column == part and place in places:
                    found.append(
                        pltpu.make_async_copy(
                            ref.at[places.index(place)],
                            block_ref.at[b, :, start : start + width],
                            sems.at[b, part],
                        )
                    )
            start += width
        return found

    def load(step):
        @pl.when((expert == 0) & (group == step))
        def _():
            for b in range(blocks):
                for copy in copies(step, b):
                    copy.start()

    for step in range(sum(len(places) for column, places in pieces if column == 0) // blocks):
        load(step)

    @pl.when(expert == 0)
    def _():
        slot_ids = lax.broadcasted_iota(jnp.int32, (capacity, rows), 0).astype(F32)
        for first in range(0, blocks, joined):
            picked = []
            for b in range(first, first + joined):
                chosen = jnp.concatenate(
                    [(slot_row_ref[b, e : e + 1, :] == slot_ids).astype(F32) for e in range(served)],
                    axis=0,
                ).astype(BF16)
                for copy in copies(0, b):
                    copy.wait()
                picked.append(dot(chosen, block_ref[b]))
            for e in range(served):
                part = [p[e * capacity : (e + 1) * capacity] for p in picked]
                taken_ref[e, first * capacity : (first + joined) * capacity] = jnp.concatenate(
                    part, axis=0
                ).astype(BF16)

    def serve(gate_ref, up_ref):
        received = taken_ref[expert]
        gate = dot(received, gate_ref[0])
        up = dot(received, up_ref[0])
        inner_ref[0] = (gate / (1.0 + jnp.exp(-gate)) * up).astype(BF16)

    @pl.when(expert < served // 2)
    def _():
        serve(own_gate_ref, own_up_ref)

    @pl.when(expert >= served // 2)
    def _():
        serve(other_gate_ref, other_up_ref)

    span = served * capacity
    lane = lax.broadcasted_iota(jnp.int32, (rows, 2 * span), 1)
    lane_expert, lane_slot = lane // capacity % served, (lane % capacity).astype(F32)
    share = blocks // served
    for i in range(share):
        b = expert * share + i
        slots, weights = slot_ref[b], weight_ref[b]
        slot = jnp.full((rows, 2 * span), -1.0, F32)
        weight = jnp.zeros((rows, 2 * span), F32)
        for e in range(served):
            slot = jnp.where(lane_expert == e, slots[:, e : e + 1], slot)
            weight = jnp.where(lane_expert == e, weights[:, e : e + 1], weight)
        high = weight.astype(BF16).astype(F32)
        spread_ref[b] = jnp.where(
            slot == lane_slot, jnp.where(lane < span, high, weight - high), 0.0
        ).astype(BF16)


def hidden_units(tokens, slots, own, other, capacity):
    devices, served, rows = slots[0].shape
    local = own[0].shape[0]
    width = own[0].shape[2]
    pieces = [(column, places) for column, places, _ in tokens]
    def own_spec(x):
        return pl.BlockSpec((1,) + x.shape[1:], lambda g, e: (jnp.minimum(e, local - 1), 0, 0))

    def other_spec(x):
        return pl.BlockSpec((1,) + x.shape[1:], lambda g, e: (jnp.maximum(e - local, 0), 0, 0))

    column_spec = pl.BlockSpec((BLOCKS_STEP, rows, served), lambda g, e: (g, 0, 0))
    return pl.pallas_call(
        functools.partial(hidden_units_kernel, capacity, pieces),
        grid=(devices // BLOCKS_STEP, served),
        in_specs=[
            pl.BlockSpec((BLOCKS_STEP, served, rows), lambda g, e: (g, 0, 0)),
            column_spec,
            column_spec,
        ]
        + [own_spec(x) for x in own]
        + [other_spec(x) for x in other]
        + [pl.BlockSpec(memory_space=pl.ANY)] * len(tokens),
        out_specs=[
            pl.BlockSpec((1, BLOCKS_STEP * capacity, width), lambda g, e: (e, g, 0)),
            pl.BlockSpec((BLOCKS_STEP, rows, 2 * served * capacity), lambda g, e: (g, 0, 0)),
        ],
        out_shape=[
            jax.ShapeDtypeStruct((served, devices * capacity, width), BF16),
            jax.ShapeDtypeStruct((devices, rows, 2 * served * capacity), BF16),
        ],
        scratch_shapes=[
            pltpu.VMEM((BLOCKS_STEP, rows, D), BF16),
            pltpu.VMEM((served, BLOCKS_STEP * capacity, D), BF16),
            pltpu.SemaphoreType.DMA((BLOCKS_STEP, len(GROUPS))),
        ],
        compiler_params=pltpu.CompilerParams(vmem_limit_bytes=56 * MIB),
        name="hidden_units",
    )(
        *slots,
        *own,
        *other,
        *[array for _, _, array in tokens],
    )


def order_places(order):
    count = len(order)
    return [
        sum(((j >> (count - 1 - k)) & 1) << bit for k, bit in enumerate(order))
        for j in range(1 << count)
    ]


def down_kernel(capacity, order, inner_ref, spread_ref, own_ref, other_ref, *refs):
    *_, keep_ref, send_ref, out_ref = refs
    served = inner_ref.shape[0]
    local = served // 2
    for e in range(served):
        down = own_ref[e] if e < local else other_ref[e - local]
        out_ref[e] = dot(inner_ref[e], down)
    places = order_places(order)
    half = len(places) // 2
    for j, place in enumerate(places):
        mine = [out_ref[e, place * capacity : (place + 1) * capacity] for e in range(served)]
        stacked = jnp.concatenate(mine, axis=0).astype(BF16)
        block = dot(spread_ref[place], jnp.concatenate([stacked, stacked], axis=0)).astype(BF16)
        if j < half:
            keep_ref[j] = block
        else:
            send_ref[j - half] = block


def down_strips(inner, spread, own, other, capacity, order, start, width, before):
    served, slots, units = inner.shape
    devices, rows, _ = spread.shape
    first = start // STRIP

    def whole(x):
        return pl.BlockSpec(x.shape, lambda i: (0, 0, 0), pipeline_mode=pl.Buffered(1))

    down_spec = pl.BlockSpec((own.shape[0], units, STRIP), lambda i: (0, 0, first + i))
    half_spec = pl.BlockSpec((devices // 2, rows, STRIP), lambda i: (0, 0, i))
    half_shape = jax.ShapeDtypeStruct((devices // 2, rows, width), BF16)
    return pl.pallas_call(
        functools.partial(down_kernel, capacity, order),
        grid=(width // STRIP,),
        in_specs=[whole(inner), whole(spread), down_spec, down_spec]
        + [pl.BlockSpec(memory_space=pl.ANY)] * len(before),
        out_specs=[half_spec, half_spec],
        out_shape=[half_shape, half_shape],
        scratch_shapes=[pltpu.VMEM((served, slots, STRIP), F32)],
        compiler_params=pltpu.CompilerParams(vmem_limit_bytes=48 * MIB),
        name="down_strips",
    )(inner, spread, own, other, *before)


def sum_by_halving(keep, send, stages):
    for stage in stages[:-1]:
        total = (keep.astype(F32) + stage_flip(send, stage).astype(F32)).astype(BF16)
        half = total.shape[0] // 2
        keep, send = total[:half], total[half:]
    return keep[0].astype(F32) + stage_flip(send, stages[-1])[0].astype(F32)


def routing(expert_ids, gate_weights, local_experts):
    outer, cores, inner = (lax.axis_size(a) for a in (("outer", "mid"), "core", "inner"))
    rows = expert_ids.shape[0]
    experts = local_experts * outer * cores * inner
    chosen = expert_ids.T[None] == jnp.arange(experts, dtype=jnp.int32)[:, None, None]
    dense = jnp.sum(jnp.where(chosen, gate_weights.T[None], 0.0), axis=1)
    by_chip = jnp.swapaxes(dense.reshape(outer, cores, inner, local_experts * rows), 1, 2)
    by_chip = by_chip.reshape(outer * inner, cores * local_experts, rows)
    return lax.all_to_all(by_chip, SAME_CORE, split_axis=0, concat_axis=0, tiled=True)


def positions(weights, local_experts):
    rows = weights.shape[2]
    turned = jnp.concatenate([weights[:, local_experts:], weights[:, :local_experts]], axis=1)
    weights = jnp.where(lax.axis_index("core") == 1, turned, weights)
    bits = weights.shape[0].bit_length() - 1
    table = jnp.asarray([order_places(order[::-1]) for order in core_orders(bits)], jnp.int32)
    source = lax.axis_index(SAME_CORE) ^ table[lax.axis_index("core")]
    weights = jnp.take(weights, source, axis=0, mode="clip")
    named = weights > 0.0
    rank = jnp.einsum(
        "set,tu->seu",
        named.astype(BF16),
        jnp.triu(jnp.ones((rows, rows), BF16)),
        preferred_element_type=F32,
    )
    slots = jnp.where(named, rank - 1.0, -1.0)
    return slots, jnp.swapaxes(slots, 1, 2), jnp.swapaxes(weights, 1, 2)


def core_orders(bits):
    first = tuple(range(bits))[::-1]
    second = tuple(first[n ^ 1] if n ^ 1 < bits else first[n] for n in range(bits))
    return first, second


def flipped(array, bit):
    devices = lax.axis_size(AXES)
    return lax.ppermute(array, AXES, [(i, i ^ bit) for i in range(devices)])


def place_flip(array, bit):
    return flipped(array, 1 << (bit if 1 << bit < lax.axis_size("inner") else bit + 1))


def over_rest(array):
    pieces = [array]
    for bit in range(lax.axis_size(REST).bit_length() - 1):
        pieces = pieces + [place_flip(piece, bit) for piece in pieces]
    return pieces


def stage_flip(array, stage):
    inner, devices = lax.axis_size("inner"), lax.axis_size(AXES)
    bits = lax.axis_size(SAME_CORE).bit_length() - 1

    def partner(i):
        bit = core_orders(bits)[i // inner % 2][stage]
        return i ^ (1 << (bit if 1 << bit < inner else bit + 1))

    return lax.ppermute(array, AXES, [(i, partner(i)) for i in range(devices)])


def send_on(pieces, chosen, stage):
    picked = [pieces[i] for i in chosen]
    places = sum((places for places, _ in picked), ())
    joined = jnp.concatenate([piece for _, piece in picked], axis=0)
    return tuple(place | (1 << stage) for place in places), stage_flip(joined, stage)


def to_everyone(array, stages, plan):
    pieces = [((0,), array[None])]
    for step, stage in enumerate(stages):
        chosen = plan[step] if step < len(plan) else [range(len(pieces))]
        pieces = pieces + [send_on(pieces, group, stage) for group in chosen]
    return pieces


def to_everyone_early(array, stages):
    pieces = [((0,), array[None])]
    pieces += [send_on(pieces, (0,), stage) for stage in (stages[0], stages[2], stages[3])]
    joined = jnp.concatenate([pieces[0][1], pieces[1][1]], axis=0)
    joined = after(joined, pieces[2][1], pieces[3][1])
    both = [(pieces[0][0] + pieces[1][0], joined)]
    pieces.append(send_on(both, (0,), stages[1]))
    pieces += [send_on(pieces, (i,), stages[2]) for i in (1, 4)]
    pieces += [send_on(pieces, group, stages[3]) for group in ((1,), (4,), (2, 5), (6,))]
    for stage in stages[4:]:
        pieces = pieces + [send_on(pieces, range(len(pieces)), stage)]
    return pieces


def shards(
    split_core,
    residual_in,
    query_input,
    key_input,
    value_input,
    out_gate,
    write_strength,
    decay_rate,
    head_gain,
    out_proj,
    post_gain,
    expert_ids,
    gate_weights,
    expert_gate,
    expert_up,
    expert_down,
):
    tok_rows = residual_in.shape[0]
    devices = lax.axis_size(AXES)
    inner_size = lax.axis_size("inner")
    local_experts = expert_gate.shape[0]
    capacity = max(2, tok_rows * TOP * 8 // (5 * local_experts * devices))
    early, late = (
        over_rest(part)[1:] for part in (out_proj[:EARLY_ROWS], out_proj[EARLY_ROWS:])
    )
    served_weights = routing(expert_ids, gate_weights, local_experts)
    other_gate, other_up, other_down = (
        flipped(x, inner_size) for x in (expert_gate, expert_up, expert_down)
    )
    maps, mix = local_terms(query_input, key_input, value_input, write_strength, decay_rate)
    maps = after(maps, *early)
    others = (other_gate, other_up, other_down)
    if split_core:
        core_early = [flipped(piece, inner_size) for piece in [out_proj] + early]
        others += tuple(core_early)
    states = entering_states(maps, devices, others, late)
    slots = positions(served_weights, local_experts)
    proj = [(out_proj,)] + list(zip(early, late))
    places = lax.axis_index(REST) ^ jnp.arange(len(proj), dtype=jnp.int32)
    if split_core:
        core = lax.axis_index("core")
        core_late = [flipped(piece, inner_size) for piece in late]
        proj += [(core_early[0],)] + list(zip(core_early[1:], core_late))
        base = places // inner_size * (2 * inner_size) + places % inner_size
        places = jnp.concatenate([base + core * inner_size, base + (1 - core) * inner_size])
    hidden, *normed = finish(
        mix, states, out_gate, head_gain, proj, places, residual_in, post_gain
    )
    bits = slots[0].shape[0].bit_length() - 1
    plain, turned = tuple(range(bits)), tuple((n + bits - 2) % bits for n in range(bits))
    plan = [[(0,)], [(0, 1)], [(0, 1, 2)], [(0, 1, 2), (3,)]]
    tokens = [(0, *piece) for piece in to_everyone_early(normed[0], plain)]
    tokens += [(1, *piece) for piece in to_everyone(normed[1], turned, plan)]
    inner, spread = hidden_units(
        tokens, slots, (expert_gate, expert_up), (other_gate, other_up), capacity
    )
    sums, start, before = [], 0, ()
    for width, stages in ((512, plain), (512, plain), (512, turned), (512, plain)):
        keep, send = down_strips(
            inner, spread, expert_down, other_down, capacity, stages[::-1], start, width, before
        )
        before = before or (keep,)
        sums.append(sum_by_halving(keep, send, stages[::-1]))
        start += width
    return (hidden.astype(F32) + jnp.concatenate(sums, axis=1)).astype(BF16)


def core_stride(devices):
    first = getattr(devices[0], "coords", None)
    for i in range(1, len(devices)):
        if first is not None and tuple(devices[i].coords) == tuple(first):
            return i
    return 1


def solution(mesh):
    devices = mesh.devices.reshape(-1)
    inner = core_stride(devices)
    columns = mesh.shape["exp"]
    if 2 * inner <= columns:
        shape, column_axes = (-1, columns // (2 * inner), 2, inner), AXES[1:]
    else:
        shape, column_axes = (-1, 1, 2, inner), ("inner",)
    split_core = "core" in column_axes
    view = Mesh(devices.reshape(shape), AXES)
    rows = P(AXES, None)
    placed = (
        (rows,) * 7 + (P(), P(None, column_axes), P(), rows, rows) + (P(AXES, None, None),) * 3
    )
    body = functools.partial(shards, split_core)
    return jax.shard_map(body, mesh=view, in_specs=placed, out_specs=rows, check_vma=False)
```

profile of v0, /device:TPU:0, one launch (start us, length us, event | category | flops | bytes accessed | tf_op | source)
XLA Modules:
  0.0 314.7 jit_solution(1146188195904330445)
XLA Ops:
  2.3 2.6 collective-permute-start
  6.2 12.4 %local_terms.1 = (bf16[16,128,384]{2,1,0:T(8,128)(2,1)S(1)}, f32[16,128,256]{2,1,0:T(8,128)S(1)}) custom-call(bf16[128,1024]{1,0:T(8,128)(2,1)S(1)} %copy-done.22, bf16[128,1024]{1,0:T(8,128)(2,1)S(1)} %copy-done.23, bf16[128,2048]{1,0:T(8,128)(2,1)S(1)} %copy-done.16, f32[4,128,4]{2,1,0:T(8,128)S(1)} %bitcast.47, f32[4,4,128]{2,1,0:T(4,128)S(1)} %bitcast.52, ...), custom_call_target="tpu_custom_call" | custom-call | tf_op jit(solution)/shard_map/local_terms/pallas_call | solution.py:151
  21.1 4.8 %collective-permute-done.refs_1_ = bf16[896,512]{1,0:T(8,128)(2,1)S(1)} collective-permute-done((bf16[896,512]{1,0:T(8,128)(2,1)S(1)}, bf16[896,512]{1,0:T(8,128)(2,1)S(1)}, u32[]{:S(2)}, u32[]{:S(2)}) %collective-permute-start) | collective-permute-done | bytes 917536 | tf_op jit(solution)/shard_map/ppermute | solution.py:567
  26.8 5.3 %all-to-all-start = ((bf16[16,128,384]{2,1,0:T(8,128)(2,1)}), bf16[16,128,384]{2,1,0:T(8,128)(2,1)}, u32[]{:S(2)}, u32[]{:S(2)}) async-start(bf16[16,128,384]{2,1,0:T(8,128)(2,1)} %after.3), calls=%async_computation | async-start | bytes 3145728 | tf_op jit(solution)/shard_map/all_to_all | solution.py:233
  32.7 2.4 slice.96
  35.1 2.5 collective-permute-done.5.refs_4_
  38.6 1.7 collective-permute-start.7
  40.2 14.8 %all-to-all-done.maps_ref = bf16[16,128,384]{2,1,0:T(8,128)(2,1)} async-done(((bf16[16,128,384]{2,1,0:T(8,128)(2,1)}), bf16[16,128,384]{2,1,0:T(8,128)(2,1)}, u32[]{:S(2)}, u32[]{:S(2)}) %all-to-all-start) | async-done | bytes 1572896 | tf_op jit(solution)/shard_map/all_to_all | solution.py:233
  56.2 4.4 %chain.1 = (f32[16,128,256]{2,1,0:T(8,128)S(1)}, f32[128,256]{1,0:T(8,128)S(1)}) custom-call(bf16[16,128,384]{2,1,0:T(8,128)(2,1)} %all-to-all-done.maps_ref, bf16[2,2048,512]{2,1,0:T(8,128)(2,1)} %collective-permute-done.1.refs_0_.other_gate_ref, bf16[2,2048,512]{2,1,0:T(8,128)(2,1)} %collective-permute-done.2.refs_1_.other_up_ref, ...), custom_call_target="tpu_custom_call" | custom-call | tf_op jit(solution)/shard_map/chain/pallas_call | solution.py:200
  62.0 4.6 %collective-permute-start.6 = (f32[128,128]{1,0:T(8,128)S(1)}, f32[128,128]{1,0:T(8,128)S(1)}, u32[]{:S(2)}, u32[]{:S(2)}) collective-permute-start(f32[128,128]{1,0:T(8,128)S(1)} %slice.95), channel_id=1, source_target_pairs={{0,16},{1,17},{2,18},{3,19},{4,20},{5,21},{6,22},{7,23},{8,24},{9,... | collective-permute-start | bytes 196616 | tf_op jit(solution)/shard_map/ppermute | solution.py:238
  66.6 13.1 %collective-permute-done.7.refs_1_.refs_2_ = bf16[1152,512]{1,0:T(8,128)(2,1)S(1)} collective-permute-done((bf16[1152,512]{1,0:T(8,128)(2,1)}, bf16[1152,512]{1,0:T(8,128)(2,1)S(1)}, u32[]{:S(2)}, u32[]{:S(2)}) %collective-permute-start.7) | collective-permute-done | bytes 1179680 | tf_op jit(solution)/shard_map/ppermute | solution.py:567
  81.4 3.0 add_convert_fusion.8
  84.5 4.3 %all-to-all-start.1 = ((bf16[16,128,128]{2,1,0:T(8,128)(2,1)}), bf16[16,128,128]{2,1,0:T(8,128)(2,1)}, u32[]{:S(2)}, u32[]{:S(2)}) async-start(bf16[16,128,128]{2,1,0:T(8,128)(2,1)} %add_convert_fusion.8), calls=%async_computation.1 | async-start | bytes 1048576 | tf_op jit(solution)/shard_map/all_to_all | solution.py:256
  88.9 10.5 %all-to-all-done.1.state_ref = bf16[16,128,128]{2,1,0:T(8,128)(2,1)} async-done(((bf16[16,128,128]{2,1,0:T(8,128)(2,1)}), bf16[16,128,128]{2,1,0:T(8,128)(2,1)}, u32[]{:S(2)}, u32[]{:S(2)}) %all-to-all-start.1) | async-done | bytes 524320 | tf_op jit(solution)/shard_map/all_to_all | solution.py:256
  102.7 5.5 %finish.1 = (bf16[128,2048]{1,0:T(8,128)(2,1)S(1)}, bf16[128,1536]{1,0:T(8,128)(2,1)S(1)}, bf16[128,512]{1,0:T(8,128)(2,1)S(1)}) custom-call(s32[4]{0:T(128)S(1)} %pad_add_fusion.place_ref, f32[16,128,256]{2,1,0:T(8,128)} %copy-done.13, bf16[16,128,128]{2,1,0:T(8,128)(2,1)} %all-to-all-done.1.state_ref, bf16[128,2048]{1,0:T(8,128)(2,1)S(1)} %copy-done.17, ...), custom_call_target="tpu_custom_call" | custom-call | tf_op jit(solution)/shard_map/finish/pallas_call | solution.py:307
  108.2 2.7 collective-permute-start.9
  111.5 9.6 %collective-permute-done.9.refs_1_ = bf16[1,128,1536]{2,1,0:T(8,128)(2,1)S(1)} collective-permute-done((bf16[1,128,1536]{2,1,0:T(8,128)(2,1)S(1)}, bf16[1,128,1536]{2,1,0:T(8,128)(2,1)S(1)}, u32[]{:S(2)}, u32[]{:S(2)}) %collective-permute-start.9) | collective-permute-done | bytes 393248 | tf_op jit(solution)/shard_map/ppermute | solution.py:589
  124.4 4.5 %all-to-all-start.2 = ((f32[16,4,128]{2,1,0:T(4,128)}), f32[16,4,128]{2,1,0:T(4,128)S(1)}, u32[]{:S(2)}, u32[]{:S(2)}) async-start(f32[16,4,128]{2,1,0:T(4,128)} %bitcast.13), calls=%async_computation.2 | async-start | bytes 65536 | tf_op jit(solution)/shard_map/all_to_all | solution.py:537
  129.0 2.0 collective-permute-start.19
  131.0 3.1 collective-permute-done.19.refs_12_
  134.1 1.9 collective-permute-start.20
  136.0 8.8 %all-to-all-done.2 = f32[16,4,128]{2,1,0:T(4,128)S(1)} async-done(((f32[16,4,128]{2,1,0:T(4,128)}), f32[16,4,128]{2,1,0:T(4,128)S(1)}, u32[]{:S(2)}, u32[]{:S(2)}) %all-to-all-start.2) | async-done | bytes 32800 | tf_op jit(solution)/shard_map/all_to_all | solution.py:537
  150.9 4.4 %collective-permute-done.13.refs_5_ = bf16[1,128,1536]{2,1,0:T(8,128)(2,1)S(1)} collective-permute-done((bf16[1,128,1536]{2,1,0:T(8,128)(2,1)S(1)}, bf16[1,128,1536]{2,1,0:T(8,128)(2,1)S(1)}, u32[]{:S(2)}, u32[]{:S(2)}) %collective-permute-start.13) | collective-permute-done | bytes 393248 | tf_op jit(solution)/shard_map/ppermute | solution.py:589
  156.3 1.8 collective-permute-start.17
  158.3 13.9 %collective-permute-done.14.refs_6_ = bf16[2,128,1536]{2,1,0:T(8,128)(2,1)} collective-permute-done((bf16[2,128,1536]{2,1,0:T(8,128)(2,1)}, bf16[2,128,1536]{2,1,0:T(8,128)(2,1)}, u32[]{:S(2)}, u32[]{:S(2)}) %collective-permute-start.14) | collective-permute-done | bytes 786464 | tf_op jit(solution)/shard_map/ppermute | solution.py:589
  172.2 1.8 collective-permute-start.18
  178.9 14.0 %collective-permute-done.22.refs_15_ = bf16[4,128,512]{2,1,0:T(8,128)(2,1)} collective-permute-done((bf16[4,128,512]{2,1,0:T(8,128)(2,1)}, bf16[4,128,512]{2,1,0:T(8,128)(2,1)}, u32[]{:S(2)}, u32[]{:S(2)}) %collective-permute-start.22) | collective-permute-done | bytes 524320 | tf_op jit(solution)/shard_map/ppermute | solution.py:589
  193.0 5.6 %collective-permute-done.23.refs_16_ = bf16[4,128,512]{2,1,0:T(8,128)(2,1)} collective-permute-done((bf16[4,128,512]{2,1,0:T(8,128)(2,1)}, bf16[4,128,512]{2,1,0:T(8,128)(2,1)}, u32[]{:S(2)}, u32[]{:S(2)}) %collective-permute-start.23) | collective-permute-done | bytes 524320 | tf_op jit(solution)/shard_map/ppermute | solution.py:589
  198.6 24.7 %hidden_units.1 = (bf16[4,512,512]{2,1,0:T(8,128)(2,1)}, bf16[16,128,256]{2,1,0:T(8,128)(2,1)}) custom-call(f32[16,4,128]{2,1,0:T(4,128)} %copy.36.slot_row_ref, f32[16,128,4]{2,1,0:T(8,128)} %bitcast_select_fusion.slot_ref, f32[16,128,4]{2,1,0:T(8,128)} %bitcast.55, bf16[2,2048,512]{2,1,0:T(8,128)(2,1)} %own_gate_ref.1, bf16[2,2048,512]{2,1,0:T(8,128)(2,1)} %own_up_ref.1, ...), custom_call_target="tpu_custom_call" | custom-call | tf_op jit(solution)/shard_map/hidden_units/pallas_call | solution.py:436
  226.1 3.5 %down_strips.4 = (bf16[8,128,512]{2,1,0:T(8,128)(2,1)S(1)}, bf16[8,128,512]{2,1,0:T(8,128)(2,1)S(1)}) custom-call(bf16[4,512,512]{2,1,0:T(8,128)(2,1)S(1)} %copy-done, bf16[16,128,256]{2,1,0:T(8,128)(2,1)S(1)} %copy-done.1, bf16[2,512,2048]{2,1,0:T(8,128)(2,1)} %own_ref.7, bf16[2,512,2048]{2,1,0:T(8,128)(2,1)} %collective-permute-done.3.refs_2_.other_ref), custom_call_target="tpu_custom_call" | custom-call | tf_op jit(solution)/shard_map/down_strips/pallas_call | solution.py:508
  230.6 4.2 %down_strips.5 = (bf16[8,128,512]{2,1,0:T(8,128)(2,1)S(1)}, bf16[8,128,512]{2,1,0:T(8,128)(2,1)S(1)}) custom-call(bf16[4,512,512]{2,1,0:T(8,128)(2,1)} %get-tuple-element.29.inner_ref, bf16[16,128,256]{2,1,0:T(8,128)(2,1)S(1)} %copy-done.2, bf16[2,512,2048]{2,1,0:T(8,128)(2,1)} %own_ref.7, bf16[2,512,2048]{2,1,0:T(8,128)(2,1)} %collective-permute-done.3.refs_2_.other_ref, ...), custom_call_target="tpu_custom_call" | custom-call | tf_op jit(solution)/shard_map/down_strips/pallas_call | solution.py:508
  235.9 4.2 %down_strips.6 = (bf16[8,128,512]{2,1,0:T(8,128)(2,1)S(1)}, bf16[8,128,512]{2,1,0:T(8,128)(2,1)S(1)}) custom-call(bf16[4,512,512]{2,1,0:T(8,128)(2,1)} %get-tuple-element.29.inner_ref, bf16[16,128,256]{2,1,0:T(8,128)(2,1)S(1)} %copy-done.2, bf16[2,512,2048]{2,1,0:T(8,128)(2,1)} %own_ref.7, bf16[2,512,2048]{2,1,0:T(8,128)(2,1)} %collective-permute-done.3.refs_2_.other_ref, ...), custom_call_target="tpu_custom_call" | custom-call | tf_op jit(solution)/shard_map/down_strips/pallas_call | solution.py:508
  240.2 4.2 %down_strips.7 = (bf16[8,128,512]{2,1,0:T(8,128)(2,1)S(1)}, bf16[8,128,512]{2,1,0:T(8,128)(2,1)S(1)}) custom-call(bf16[4,512,512]{2,1,0:T(8,128)(2,1)} %get-tuple-element.29.inner_ref, bf16[16,128,256]{2,1,0:T(8,128)(2,1)S(1)} %copy-done.2, bf16[2,512,2048]{2,1,0:T(8,128)(2,1)} %own_ref.7, bf16[2,512,2048]{2,1,0:T(8,128)(2,1)} %collective-permute-done.3.refs_2_.other_ref, ...), custom_call_target="tpu_custom_call" | custom-call | tf_op jit(solution)/shard_map/down_strips/pallas_call | solution.py:508
  245.4 3.2 %collective-permute-done.24 = bf16[8,128,512]{2,1,0:T(8,128)(2,1)S(1)} collective-permute-done((bf16[8,128,512]{2,1,0:T(8,128)(2,1)S(1)}, bf16[8,128,512]{2,1,0:T(8,128)(2,1)S(1)}, u32[]{:S(2)}, u32[]{:S(2)}) %collective-permute-start.24) | collective-permute-done | bytes 1048608 | tf_op jit(solution)/shard_map/ppermute | solution.py:589
  249.0 2.5 collective-permute-start.25
  251.5 16.1 %collective-permute-done.28 = bf16[8,128,512]{2,1,0:T(8,128)(2,1)S(1)} collective-permute-done((bf16[8,128,512]{2,1,0:T(8,128)(2,1)S(1)}, bf16[8,128,512]{2,1,0:T(8,128)(2,1)S(1)}, u32[]{:S(2)}, u32[]{:S(2)}) %collective-permute-start.28) | collective-permute-done | bytes 1048608 | tf_op jit(solution)/shard_map/ppermute | solution.py:589
  267.9 2.3 collective-permute-start.29
  270.2 1.6 collective-permute-done.32
  272.2 6.3 %collective-permute-start.33 = (bf16[4,128,512]{2,1,0:T(8,128)(2,1)S(1)}, bf16[4,128,512]{2,1,0:T(8,128)(2,1)S(1)}, u32[]{:S(2)}, u32[]{:S(2)}) collective-permute-start(bf16[4,128,512]{2,1,0:T(8,128)(2,1)S(1)} %slice.141), channel_id=1, source_target_pairs={{0,16},{1,9},{2,18},{3,11},{4,20},{5,13},{6,22},{7,15},{8,24},{9,1... | collective-permute-start | bytes 1572872 | tf_op jit(solution)/shard_map/ppermute | solution.py:589
  278.5 6.0 %collective-permute-done.36 = bf16[8,128,512]{2,1,0:T(8,128)(2,1)S(1)} collective-permute-done((bf16[8,128,512]{2,1,0:T(8,128)(2,1)S(1)}, bf16[8,128,512]{2,1,0:T(8,128)(2,1)S(1)}, u32[]{:S(2)}, u32[]{:S(2)}) %collective-permute-start.36) | collective-permute-done | bytes 1048608 | tf_op jit(solution)/shard_map/ppermute | solution.py:589
  284.9 1.7 collective-permute-start.37
  287.0 2.1 collective-permute-start.30
  289.0 8.0 %collective-permute-done.33 = bf16[4,128,512]{2,1,0:T(8,128)(2,1)S(1)} collective-permute-done((bf16[4,128,512]{2,1,0:T(8,128)(2,1)S(1)}, bf16[4,128,512]{2,1,0:T(8,128)(2,1)S(1)}, u32[]{:S(2)}, u32[]{:S(2)}) %collective-permute-start.33) | collective-permute-done | bytes 524320 | tf_op jit(solution)/shard_map/ppermute | solution.py:589
  298.6 1.7 collective-permute-start.27
  300.3 2.2 collective-permute-done.30
  305.1 1.6 collective-permute-done.38
  306.9 2.7 collective-permute-done.31
  309.7 4.0 %collective-permute-done.39 = bf16[1,128,512]{2,1,0:T(8,128)(2,1)S(1)} collective-permute-done((bf16[1,128,512]{2,1,0:T(8,128)(2,1)S(1)}, bf16[1,128,512]{2,1,0:T(8,128)(2,1)S(1)}, u32[]{:S(2)}, u32[]{:S(2)}) %collective-permute-start.39) | collective-permute-done | bytes 131104 | tf_op jit(solution)/shard_map/ppermute | solution.py:589
  (186 shorter events, 45.1 us)
Async XLA Ops:
  0.0 55.0 %collective-permute-start.3 = (bf16[2,512,2048]{2,1,0:T(8,128)(2,1)}, bf16[2,512,2048]{2,1,0:T(8,128)(2,1)}, u32[]{:S(2)}, u32[]{:S(2)}) collective-permute-start(bf16[2,512,2048]{2,1,0:T(8,128)(2,1)} %own_ref.7), channel_id=1, source_target_pairs={{0,1},{1,0},{2,3},{3,2},{4,5},{5,4},{6,7},{7,6},{8,9},{9,8},{10,11... | collective-permute-start | bytes 12582920 | tf_op jit(solution)/shard_map/ppermute | solution.py:567
  0.5 54.5 %collective-permute-start.1 = (bf16[2,2048,512]{2,1,0:T(8,128)(2,1)}, bf16[2,2048,512]{2,1,0:T(8,128)(2,1)}, u32[]{:S(2)}, u32[]{:S(2)}) collective-permute-start(bf16[2,2048,512]{2,1,0:T(8,128)(2,1)} %own_gate_ref.1), channel_id=1, source_target_pairs={{0,1},{1,0},{2,3},{3,2},{4,5},{5,4},{6,7},{7,6},{8,9},{9,8},{10,11... | collective-permute-start | bytes 12582920 | tf_op jit(solution)/shard_map/ppermute | solution.py:567
  0.6 54.4 %collective-permute-start.2 = (bf16[2,2048,512]{2,1,0:T(8,128)(2,1)}, bf16[2,2048,512]{2,1,0:T(8,128)(2,1)}, u32[]{:S(2)}, u32[]{:S(2)}) collective-permute-start(bf16[2,2048,512]{2,1,0:T(8,128)(2,1)} %own_up_ref.1), channel_id=1, source_target_pairs={{0,1},{1,0},{2,3},{3,2},{4,5},{5,4},{6,7},{7,6},{8,9},{9,8},{10,11... | collective-permute-start | bytes 12582920 | tf_op jit(solution)/shard_map/ppermute | solution.py:567
  2.3 23.6 %collective-permute-start = (bf16[896,512]{1,0:T(8,128)(2,1)S(1)}, bf16[896,512]{1,0:T(8,128)(2,1)S(1)}, u32[]{:S(2)}, u32[]{:S(2)}) collective-permute-start(bf16[896,512]{1,0:T(8,128)(2,1)S(1)} %slice.93), channel_id=1, source_target_pairs={{0,2},{1,3},{2,0},{3,1},{4,6},{5,7},{6,4},{7,5},{8,10},{9,11},{10,... | collective-permute-start | bytes 2752520 | tf_op jit(solution)/shard_map/ppermute | solution.py:567
  26.8 28.2 %all-to-all-start = ((bf16[16,128,384]{2,1,0:T(8,128)(2,1)}), bf16[16,128,384]{2,1,0:T(8,128)(2,1)}, u32[]{:S(2)}, u32[]{:S(2)}) async-start(bf16[16,128,384]{2,1,0:T(8,128)(2,1)} %after.3), calls=%async_computation | async-start | bytes 3145728 | tf_op jit(solution)/shard_map/all_to_all | solution.py:233
  32.1 8.1 %collective-permute-start.4 = (bf16[2048,512]{1,0:T(8,128)(2,1)}, bf16[2048,512]{1,0:T(8,128)(2,1)S(1)}, u32[]{:S(2)}, u32[]{:S(2)}) collective-permute-start(bf16[2048,512]{1,0:T(8,128)(2,1)} %refs_0_.1), channel_id=1, source_target_pairs={{0,1},{1,0},{2,3},{3,2},{4,5},{5,4},{6,7},{7,6},{8,9},{9,8},{10,11... | collective-permute-start | bytes 6291464 | tf_op jit(solution)/shard_map/ppermute | solution.py:567
  32.5 5.2 %collective-permute-start.5 = (bf16[896,512]{1,0:T(8,128)(2,1)S(1)}, bf16[896,512]{1,0:T(8,128)(2,1)S(1)}, u32[]{:S(2)}, u32[]{:S(2)}) collective-permute-start(bf16[896,512]{1,0:T(8,128)(2,1)S(1)} %copy-done.8), channel_id=1, source_target_pairs={{0,1},{1,0},{2,3},{3,2},{4,5},{5,4},{6,7},{7,6},{8,9},{9,8},{10,11... | collective-permute-start | bytes 2752520 | tf_op jit(solution)/shard_map/ppermute | solution.py:567
  38.6 41.2 %collective-permute-start.7 = (bf16[1152,512]{1,0:T(8,128)(2,1)}, bf16[1152,512]{1,0:T(8,128)(2,1)S(1)}, u32[]{:S(2)}, u32[]{:S(2)}) collective-permute-start(bf16[1152,512]{1,0:T(8,128)(2,1)} %slice.96), channel_id=1, source_target_pairs={{0,2},{1,3},{2,0},{3,1},{4,6},{5,7},{6,4},{7,5},{8,10},{9,11},{10,... | collective-permute-start | bytes 3538952 | tf_op jit(solution)/shard_map/ppermute | solution.py:567
  62.0 37.4 %copy-start.25 = (f32[2048]{0:T(1024)S(1)}, f32[2048]{0:T(1024)}, u32[]{:S(2)}) copy-start(f32[2048]{0:T(1024)} %param.25) | copy-start | bytes 24580
  62.0 37.4 %copy-start.26 = (f32[128]{0:T(128)S(1)}, f32[128]{0:T(128)}, u32[]{:S(2)}) copy-start(f32[128]{0:T(128)} %param.23) | copy-start | bytes 1540
  62.0 37.4 %copy-start.9 = (bf16[896,512]{1,0:T(8,128)(2,1)S(1)}, bf16[896,512]{1,0:T(8,128)(2,1)}, u32[]{:S(2)}) copy-start(bf16[896,512]{1,0:T(8,128)(2,1)} %copy-done.7) | copy-start | bytes 2752516
  62.0 17.8 %collective-permute-start.6 = (f32[128,128]{1,0:T(8,128)S(1)}, f32[128,128]{1,0:T(8,128)S(1)}, u32[]{:S(2)}, u32[]{:S(2)}) collective-permute-start(f32[128,128]{1,0:T(8,128)S(1)} %slice.95), channel_id=1, source_target_pairs={{0,16},{1,17},{2,18},{3,19},{4,20},{5,21},{6,22},{7,23},{8,24},{9,... | collective-permute-start | bytes 196616 | tf_op jit(solution)/shard_map/ppermute | solution.py:238
  79.8 9.1 %collective-permute-start.8 = (bf16[1152,512]{1,0:T(8,128)(2,1)S(1)}, bf16[1152,512]{1,0:T(8,128)(2,1)}, u32[]{:S(2)}, u32[]{:S(2)}) collective-permute-start(bf16[1152,512]{1,0:T(8,128)(2,1)S(1)} %collective-permute-done.7.refs_1_.refs_2_), channel_id=1, source_target_pairs={{0,1},{1,0},{2,3},{3,2},{4,5},{5,4},{6,7},{7,6},{8,9},{9,8},{10,11... | collective-permute-start | bytes 3538952 | tf_op jit(solution)/shard_map/ppermute | solution.py:567
  84.5 14.9 %all-to-all-start.1 = ((bf16[16,128,128]{2,1,0:T(8,128)(2,1)}), bf16[16,128,128]{2,1,0:T(8,128)(2,1)}, u32[]{:S(2)}, u32[]{:S(2)}) async-start(bf16[16,128,128]{2,1,0:T(8,128)(2,1)} %add_convert_fusion.8), calls=%async_computation.1 | async-start | bytes 1048576 | tf_op jit(solution)/shard_map/all_to_all | solution.py:256
  108.2 39.7 %copy-start.15 = (bf16[128,512]{1,0:T(8,128)(2,1)}, bf16[128,512]{1,0:T(8,128)(2,1)S(1)}, u32[]{:S(2)}) copy-start(bf16[128,512]{1,0:T(8,128)(2,1)S(1)} %get-tuple-element.28) | copy-start | bytes 393220
  108.2 13.0 %collective-permute-start.9 = (bf16[1,128,1536]{2,1,0:T(8,128)(2,1)S(1)}, bf16[1,128,1536]{2,1,0:T(8,128)(2,1)S(1)}, u32[]{:S(2)}, u32[]{:S(2)}) collective-permute-start(bf16[1,128,1536]{2,1,0:T(8,128)(2,1)S(1)} %bitcast.38), channel_id=1, source_target_pairs={{0,16},{1,9},{2,18},{3,11},{4,20},{5,13},{6,22},{7,15},{8,24},{9,1... | collective-permute-start | bytes 1179656 | tf_op jit(solution)/shard_map/ppermute | solution.py:589
  110.9 11.3 %collective-permute-start.10 = (bf16[1,128,1536]{2,1,0:T(8,128)(2,1)S(1)}, bf16[1,128,1536]{2,1,0:T(8,128)(2,1)S(1)}, u32[]{:S(2)}, u32[]{:S(2)}) collective-permute-start(bf16[1,128,1536]{2,1,0:T(8,128)(2,1)S(1)} %bitcast.39), channel_id=1, source_target_pairs={{0,4},{1,3},{2,6},{3,1},{4,0},{5,7},{6,2},{7,5},{8,12},{9,11},{10,... | collective-permute-start | bytes 1179656 | tf_op jit(solution)/shard_map/ppermute | solution.py:589
  110.9 11.3 %collective-permute-start.11 = (bf16[1,128,1536]{2,1,0:T(8,128)(2,1)S(1)}, bf16[1,128,1536]{2,1,0:T(8,128)(2,1)S(1)}, u32[]{:S(2)}, u32[]{:S(2)}) collective-permute-start(bf16[1,128,1536]{2,1,0:T(8,128)(2,1)S(1)} %bitcast.40), channel_id=1, source_target_pairs={{0,2},{1,5},{2,0},{3,7},{4,6},{5,1},{6,4},{7,3},{8,10},{9,13},{10,... | collective-permute-start | bytes 1179656 | tf_op jit(solution)/shard_map/ppermute | solution.py:589
  123.7 22.6 %collective-permute-start.12 = (bf16[2,128,1536]{2,1,0:T(8,128)(2,1)}, bf16[2,128,1536]{2,1,0:T(8,128)(2,1)}, u32[]{:S(2)}, u32[]{:S(2)}) collective-permute-start(bf16[2,128,1536]{2,1,0:T(8,128)(2,1)} %after.5), channel_id=1, source_target_pairs={{0,8},{1,17},{2,10},{3,19},{4,12},{5,21},{6,14},{7,23},{8,0},{9,25... | collective-permute-start | bytes 2359304 | tf_op jit(solution)/shard_map/ppermute | solution.py:589
  124.4 20.3 %all-to-all-start.2 = ((f32[16,4,128]{2,1,0:T(4,128)}), f32[16,4,128]{2,1,0:T(4,128)S(1)}, u32[]{:S(2)}, u32[]{:S(2)}) async-start(f32[16,4,128]{2,1,0:T(4,128)} %bitcast.13), calls=%async_computation.2 | async-start | bytes 65536 | tf_op jit(solution)/shard_map/all_to_all | solution.py:537
  129.0 5.1 %collective-permute-start.19 = (bf16[1,128,512]{2,1,0:T(8,128)(2,1)S(1)}, bf16[1,128,512]{2,1,0:T(8,128)(2,1)S(1)}, u32[]{:S(2)}, u32[]{:S(2)}) collective-permute-start(bf16[1,128,512]{2,1,0:T(8,128)(2,1)S(1)} %bitcast.43), channel_id=1, source_target_pairs={{0,4},{1,3},{2,6},{3,1},{4,0},{5,7},{6,2},{7,5},{8,12},{9,11},{10,... | collective-permute-start | bytes 393224 | tf_op jit(solution)/shard_map/ppermute | solution.py:589
  134.1 13.8 %collective-permute-start.20 = (bf16[2,128,512]{2,1,0:T(8,128)(2,1)S(1)}, bf16[2,128,512]{2,1,0:T(8,128)(2,1)S(1)}, u32[]{:S(2)}, u32[]{:S(2)}) collective-permute-start(bf16[2,128,512]{2,1,0:T(8,128)(2,1)S(1)} %pad_maximum_fusion.3), channel_id=1, source_target_pairs={{0,2},{1,5},{2,0},{3,7},{4,6},{5,1},{6,4},{7,3},{8,10},{9,13},{10,... | collective-permute-start | bytes 786440 | tf_op jit(solution)/shard_map/ppermute | solution.py:589
  144.8 10.5 %collective-permute-start.13 = (bf16[1,128,1536]{2,1,0:T(8,128)(2,1)S(1)}, bf16[1,128,1536]{2,1,0:T(8,128)(2,1)S(1)}, u32[]{:S(2)}, u32[]{:S(2)}) collective-permute-start(bf16[1,128,1536]{2,1,0:T(8,128)(2,1)S(1)} %collective-permute-done.9.refs_1_), channel_id=1, source_target_pairs={{0,4},{1,3},{2,6},{3,1},{4,0},{5,7},{6,2},{7,5},{8,12},{9,11},{10,... | collective-permute-start | bytes 1179656 | tf_op jit(solution)/shard_map/ppermute | solution.py:589
  146.3 25.9 %collective-permute-start.14 = (bf16[2,128,1536]{2,1,0:T(8,128)(2,1)}, bf16[2,128,1536]{2,1,0:T(8,128)(2,1)}, u32[]{:S(2)}, u32[]{:S(2)}) collective-permute-start(bf16[2,128,1536]{2,1,0:T(8,128)(2,1)} %collective-permute-done.12.refs_4_), channel_id=1, source_target_pairs={{0,4},{1,3},{2,6},{3,1},{4,0},{5,7},{6,2},{7,5},{8,12},{9,11},{10,... | collective-permute-start | bytes 2359304 | tf_op jit(solution)/shard_map/ppermute | solution.py:589
  147.9 29.9 %copy-start.27 = (f32[16,4,128]{1,2,0:T(8,128)}, f32[16,4,128]{1,2,0:T(8,128)S(1)}, u32[]{:S(2)}) copy-start(f32[16,4,128]{1,2,0:T(8,128)S(1)} %copy.32) | copy-start | bytes 98308
  148.8 25.9 %collective-permute-start.21 = (bf16[4,128,512]{2,1,0:T(8,128)(2,1)}, bf16[4,128,512]{2,1,0:T(8,128)(2,1)}, u32[]{:S(2)}, u32[]{:S(2)}) collective-permute-start(bf16[4,128,512]{2,1,0:T(8,128)(2,1)} %pad_maximum_fusion.2), channel_id=1, source_target_pairs={{0,16},{1,9},{2,18},{3,11},{4,20},{5,13},{6,22},{7,15},{8,24},{9,1... | collective-permute-start | bytes 1572872 | tf_op jit(solution)/shard_map/ppermute | solution.py:589
  149.7 24.9 %collective-permute-start.15 = (bf16[1,128,1536]{2,1,0:T(8,128)(2,1)S(1)}, bf16[1,128,1536]{2,1,0:T(8,128)(2,1)S(1)}, u32[]{:S(2)}, u32[]{:S(2)}) collective-permute-start(bf16[1,128,1536]{2,1,0:T(8,128)(2,1)S(1)} %collective-permute-done.9.refs_1_), channel_id=1, source_target_pairs={{0,2},{1,5},{2,0},{3,7},{4,6},{5,1},{6,4},{7,3},{8,10},{9,13},{10,... | collective-permute-start | bytes 1179656 | tf_op jit(solution)/shard_map/ppermute | solution.py:589
  156.3 42.3 %collective-permute-start.17 = (bf16[2,128,1536]{2,1,0:T(8,128)(2,1)}, bf16[2,128,1536]{2,1,0:T(8,128)(2,1)}, u32[]{:S(2)}, u32[]{:S(2)}) collective-permute-start(bf16[2,128,1536]{2,1,0:T(8,128)(2,1)} %pad_maximum_fusion.1), channel_id=1, source_target_pairs={{0,2},{1,5},{2,0},{3,7},{4,6},{5,1},{6,4},{7,3},{8,10},{9,13},{10,... | collective-permute-start | bytes 2359304 | tf_op jit(solution)/shard_map/ppermute | solution.py:589
  158.1 40.5 %collective-permute-start.16 = (bf16[2,128,1536]{2,1,0:T(8,128)(2,1)}, bf16[2,128,1536]{2,1,0:T(8,128)(2,1)}, u32[]{:S(2)}, u32[]{:S(2)}) collective-permute-start(bf16[2,128,1536]{2,1,0:T(8,128)(2,1)} %collective-permute-done.12.refs_4_), channel_id=1, source_target_pairs={{0,2},{1,5},{2,0},{3,7},{4,6},{5,1},{6,4},{7,3},{8,10},{9,13},{10,... | collective-permute-start | bytes 2359304 | tf_op jit(solution)/shard_map/ppermute | solution.py:589
  172.2 26.4 %collective-permute-start.18 = (bf16[2,128,1536]{2,1,0:T(8,128)(2,1)}, bf16[2,128,1536]{2,1,0:T(8,128)(2,1)}, u32[]{:S(2)}, u32[]{:S(2)}) collective-permute-start(bf16[2,128,1536]{2,1,0:T(8,128)(2,1)} %collective-permute-done.14.refs_6_), channel_id=1, source_target_pairs={{0,2},{1,5},{2,0},{3,7},{4,6},{5,1},{6,4},{7,3},{8,10},{9,13},{10,... | collective-permute-start | bytes 2359304 | tf_op jit(solution)/shard_map/ppermute | solution.py:589
  174.6 18.3 %collective-permute-start.22 = (bf16[4,128,512]{2,1,0:T(8,128)(2,1)}, bf16[4,128,512]{2,1,0:T(8,128)(2,1)}, u32[]{:S(2)}, u32[]{:S(2)}) collective-permute-start(bf16[4,128,512]{2,1,0:T(8,128)(2,1)} %pad_maximum_fusion.2), channel_id=1, source_target_pairs={{0,8},{1,17},{2,10},{3,19},{4,12},{5,21},{6,14},{7,23},{8,0},{9,25... | collective-permute-start | bytes 1572872 | tf_op jit(solution)/shard_map/ppermute | solution.py:589
  175.4 23.2 %collective-permute-start.23 = (bf16[4,128,512]{2,1,0:T(8,128)(2,1)}, bf16[4,128,512]{2,1,0:T(8,128)(2,1)}, u32[]{:S(2)}, u32[]{:S(2)}) collective-permute-start(bf16[4,128,512]{2,1,0:T(8,128)(2,1)} %collective-permute-done.21.refs_14_), channel_id=1, source_target_pairs={{0,8},{1,17},{2,10},{3,19},{4,12},{5,21},{6,14},{7,23},{8,0},{9,25... | collective-permute-start | bytes 1572872 | tf_op jit(solution)/shard_map/ppermute | solution.py:589
  229.6 19.1 %collective-permute-start.24 = (bf16[8,128,512]{2,1,0:T(8,128)(2,1)S(1)}, bf16[8,128,512]{2,1,0:T(8,128)(2,1)S(1)}, u32[]{:S(2)}, u32[]{:S(2)}) collective-permute-start(bf16[8,128,512]{2,1,0:T(8,128)(2,1)S(1)} %get-tuple-element.32), channel_id=1, source_target_pairs={{0,2},{1,5},{2,0},{3,7},{4,6},{5,1},{6,4},{7,3},{8,10},{9,13},{10,... | collective-permute-start | bytes 3145736 | tf_op jit(solution)/shard_map/ppermute | solution.py:589
  234.8 32.8 %collective-permute-start.28 = (bf16[8,128,512]{2,1,0:T(8,128)(2,1)S(1)}, bf16[8,128,512]{2,1,0:T(8,128)(2,1)S(1)}, u32[]{:S(2)}, u32[]{:S(2)}) collective-permute-start(bf16[8,128,512]{2,1,0:T(8,128)(2,1)S(1)} %get-tuple-element.34), channel_id=1, source_target_pairs={{0,2},{1,5},{2,0},{3,7},{4,6},{5,1},{6,4},{7,3},{8,10},{9,13},{10,... | collective-permute-start | bytes 3145736 | tf_op jit(solution)/shard_map/ppermute | solution.py:589
  240.2 31.7 %collective-permute-start.32 = (bf16[8,128,512]{2,1,0:T(8,128)(2,1)S(1)}, bf16[8,128,512]{2,1,0:T(8,128)(2,1)S(1)}, u32[]{:S(2)}, u32[]{:S(2)}) collective-permute-start(bf16[8,128,512]{2,1,0:T(8,128)(2,1)S(1)} %get-tuple-element.36), channel_id=1, source_target_pairs={{0,8},{1,17},{2,10},{3,19},{4,12},{5,21},{6,14},{7,23},{8,0},{9,25... | collective-permute-start | bytes 3145736 | tf_op jit(solution)/shard_map/ppermute | solution.py:589
  244.4 40.1 %collective-permute-start.36 = (bf16[8,128,512]{2,1,0:T(8,128)(2,1)S(1)}, bf16[8,128,512]{2,1,0:T(8,128)(2,1)S(1)}, u32[]{:S(2)}, u32[]{:S(2)}) collective-permute-start(bf16[8,128,512]{2,1,0:T(8,128)(2,1)S(1)} %get-tuple-element.38), channel_id=1, source_target_pairs={{0,2},{1,5},{2,0},{3,7},{4,6},{5,1},{6,4},{7,3},{8,10},{9,13},{10,... | collective-permute-start | bytes 3145736 | tf_op jit(solution)/shard_map/ppermute | solution.py:589
  249.0 37.6 %collective-permute-start.25 = (bf16[4,128,512]{2,1,0:T(8,128)(2,1)S(1)}, bf16[4,128,512]{2,1,0:T(8,128)(2,1)S(1)}, u32[]{:S(2)}, u32[]{:S(2)}) collective-permute-start(bf16[4,128,512]{2,1,0:T(8,128)(2,1)S(1)} %slice.129), channel_id=1, source_target_pairs={{0,4},{1,3},{2,6},{3,1},{4,0},{5,7},{6,2},{7,5},{8,12},{9,11},{10,... | collective-permute-start | bytes 1572872 | tf_op jit(solution)/shard_map/ppermute | solution.py:589
  267.9 18.9 %collective-permute-start.29 = (bf16[4,128,512]{2,1,0:T(8,128)(2,1)S(1)}, bf16[4,128,512]{2,1,0:T(8,128)(2,1)S(1)}, u32[]{:S(2)}, u32[]{:S(2)}) collective-permute-start(bf16[4,128,512]{2,1,0:T(8,128)(2,1)S(1)} %slice.135), channel_id=1, source_target_pairs={{0,4},{1,3},{2,6},{3,1},{4,0},{5,7},{6,2},{7,5},{8,12},{9,11},{10,... | collective-permute-start | bytes 1572872 | tf_op jit(solution)/shard_map/ppermute | solution.py:589
  272.2 24.8 %collective-permute-start.33 = (bf16[4,128,512]{2,1,0:T(8,128)(2,1)S(1)}, bf16[4,128,512]{2,1,0:T(8,128)(2,1)S(1)}, u32[]{:S(2)}, u32[]{:S(2)}) collective-permute-start(bf16[4,128,512]{2,1,0:T(8,128)(2,1)S(1)} %slice.141), channel_id=1, source_target_pairs={{0,16},{1,9},{2,18},{3,11},{4,20},{5,13},{6,22},{7,15},{8,24},{9,1... | collective-permute-start | bytes 1572872 | tf_op jit(solution)/shard_map/ppermute | solution.py:589
  284.9 13.3 %collective-permute-start.37 = (bf16[4,128,512]{2,1,0:T(8,128)(2,1)S(1)}, bf16[4,128,512]{2,1,0:T(8,128)(2,1)S(1)}, u32[]{:S(2)}, u32[]{:S(2)}) collective-permute-start(bf16[4,128,512]{2,1,0:T(8,128)(2,1)S(1)} %slice.147), channel_id=1, source_target_pairs={{0,4},{1,3},{2,6},{3,1},{4,0},{5,7},{6,2},{7,5},{8,12},{9,11},{10,... | collective-permute-start | bytes 1572872 | tf_op jit(solution)/shard_map/ppermute | solution.py:589
  286.7 11.8 %collective-permute-start.26 = (bf16[2,128,512]{2,1,0:T(8,128)(2,1)S(1)}, bf16[2,128,512]{2,1,0:T(8,128)(2,1)S(1)}, u32[]{:S(2)}, u32[]{:S(2)}) collective-permute-start(bf16[2,128,512]{2,1,0:T(8,128)(2,1)S(1)} %slice.131), channel_id=1, source_target_pairs={{0,8},{1,17},{2,10},{3,19},{4,12},{5,21},{6,14},{7,23},{8,0},{9,25... | collective-permute-start | bytes 786440 | tf_op jit(solution)/shard_map/ppermute | solution.py:589
  287.0 15.5 %collective-permute-start.30 = (bf16[2,128,512]{2,1,0:T(8,128)(2,1)S(1)}, bf16[2,128,512]{2,1,0:T(8,128)(2,1)S(1)}, u32[]{:S(2)}, u32[]{:S(2)}) collective-permute-start(bf16[2,128,512]{2,1,0:T(8,128)(2,1)S(1)} %slice.137), channel_id=1, source_target_pairs={{0,8},{1,17},{2,10},{3,19},{4,12},{5,21},{6,14},{7,23},{8,0},{9,25... | collective-permute-start | bytes 786440 | tf_op jit(solution)/shard_map/ppermute | solution.py:589
  297.2 6.4 %collective-permute-start.34 = (bf16[2,128,512]{2,1,0:T(8,128)(2,1)S(1)}, bf16[2,128,512]{2,1,0:T(8,128)(2,1)S(1)}, u32[]{:S(2)}, u32[]{:S(2)}) collective-permute-start(bf16[2,128,512]{2,1,0:T(8,128)(2,1)S(1)} %slice.143), channel_id=1, source_target_pairs={{0,2},{1,5},{2,0},{3,7},{4,6},{5,1},{6,4},{7,3},{8,10},{9,13},{10,... | collective-permute-start | bytes 786440 | tf_op jit(solution)/shard_map/ppermute | solution.py:589
  298.4 8.3 %collective-permute-start.38 = (bf16[2,128,512]{2,1,0:T(8,128)(2,1)S(1)}, bf16[2,128,512]{2,1,0:T(8,128)(2,1)S(1)}, u32[]{:S(2)}, u32[]{:S(2)}) collective-permute-start(bf16[2,128,512]{2,1,0:T(8,128)(2,1)S(1)} %slice.149), channel_id=1, source_target_pairs={{0,8},{1,17},{2,10},{3,19},{4,12},{5,21},{6,14},{7,23},{8,0},{9,25... | collective-permute-start | bytes 786440 | tf_op jit(solution)/shard_map/ppermute | solution.py:589
  298.6 8.3 %collective-permute-start.27 = (bf16[1,128,512]{2,1,0:T(8,128)(2,1)S(1)}, bf16[1,128,512]{2,1,0:T(8,128)(2,1)S(1)}, u32[]{:S(2)}, u32[]{:S(2)}) collective-permute-start(bf16[1,128,512]{2,1,0:T(8,128)(2,1)S(1)} %slice.133), channel_id=1, source_target_pairs={{0,16},{1,9},{2,18},{3,11},{4,20},{5,13},{6,22},{7,15},{8,24},{9,1... | collective-permute-start | bytes 393224 | tf_op jit(solution)/shard_map/ppermute | solution.py:589
  302.6 7.1 %collective-permute-start.31 = (bf16[1,128,512]{2,1,0:T(8,128)(2,1)S(1)}, bf16[1,128,512]{2,1,0:T(8,128)(2,1)S(1)}, u32[]{:S(2)}, u32[]{:S(2)}) collective-permute-start(bf16[1,128,512]{2,1,0:T(8,128)(2,1)S(1)} %slice.139), channel_id=1, source_target_pairs={{0,16},{1,9},{2,18},{3,11},{4,20},{5,13},{6,22},{7,15},{8,24},{9,1... | collective-permute-start | bytes 393224 | tf_op jit(solution)/shard_map/ppermute | solution.py:589
  303.7 6.0 %collective-permute-start.35 = (bf16[1,128,512]{2,1,0:T(8,128)(2,1)S(1)}, bf16[1,128,512]{2,1,0:T(8,128)(2,1)S(1)}, u32[]{:S(2)}, u32[]{:S(2)}) collective-permute-start(bf16[1,128,512]{2,1,0:T(8,128)(2,1)S(1)} %slice.145), channel_id=1, source_target_pairs={{0,4},{1,3},{2,6},{3,1},{4,0},{5,7},{6,2},{7,5},{8,12},{9,11},{10,... | collective-permute-start | bytes 393224 | tf_op jit(solution)/shard_map/ppermute | solution.py:589
  306.8 7.0 %collective-permute-start.39 = (bf16[1,128,512]{2,1,0:T(8,128)(2,1)S(1)}, bf16[1,128,512]{2,1,0:T(8,128)(2,1)S(1)}, u32[]{:S(2)}, u32[]{:S(2)}) collective-permute-start(bf16[1,128,512]{2,1,0:T(8,128)(2,1)S(1)} %slice.151), channel_id=1, source_target_pairs={{0,16},{1,9},{2,18},{3,11},{4,20},{5,13},{6,22},{7,15},{8,24},{9,1... | collective-permute-start | bytes 393224 | tf_op jit(solution)/shard_map/ppermute | solution.py:589
  (35 other events, 279.8 us)
where the time goes:
time: 315 us
  waiting for transfers between devices  151 us (48%)
  starting transfers between devices  63.7 us (20%)
  Pallas kernels  63 us (20%)
  local copies, waits for them, and re-layouts  23.7 us (8%)
  other arithmetic  8.19 us (3%)
  matrix products  4.1 us (1%)
    ppermute x31, waiting for transfers between devices, stage_flip(): return lax.ppermute(array, AXES, [(i, partner(i)) for i in range(devices)])  96.8 us
    ppermute x31, starting transfers between devices, stage_flip(): return lax.ppermute(array, AXES, [(i, partner(i)) for i in range(devices)])  39.1 us
    pallas_call x1, Pallas kernels, hidden_units(): pl.pallas_call(functools.partial(hidden_units_kernel, capacity, pieces),...  24.7 us
    ppermute x8, waiting for transfers between devices, flipped(): return lax.ppermute(array, AXES, [(i, i ^ bit) for i in range(devices)])  20.4 us
    unnamed x80, local copies, waits for them, and re-layouts  16.8 us
    pallas_call x4, Pallas kernels, down_strips(): pl.pallas_call(functools.partial(down_kernel, capacity, order), grid=(wid...  16.1 us
    all_to_all x1, waiting for transfers between devices, entering_states(): lax.all_to_all(maps, AXES, split_axis=0, concat_axis=0, axis_index_groups...  14.8 us
    pallas_call x1, Pallas kernels, local_terms(): pl.pallas_call(local_kernel, grid=(groups,), in_specs=[pl.BlockSpec((n, w...  12.4 us
  transfers between devices with their start and end apart: 43, of which 23 were waited for; matrix products, arithmetic and copies ran while one was open for 6% of the time, Pallas kernels for 9%

commit v1 on v0

--- a/solution.py
+++ b/solution.py
@@ -17,7 +17,7 @@
 BLOCKS_STEP = 16
 GROUPS = (1536, 512)
 STRIP = 256
-EARLY_ROWS = 896
+EARLY_ROWS = 768
 
 F32 = jnp.float32
 BF16 = jnp.bfloat16
@@ -226,7 +226,7 @@
     )(array, *others)
 
 
-def entering_states(maps, devices, others, late):
+def entering_states(maps, devices, others, late, route):
     heads = maps.shape[0]
     segments = devices // heads
     groups = [[g * heads + h for h in range(heads)] for g in range(segments)]
@@ -246,7 +246,8 @@
         for g in range(2, segments):
             carry = adds[g - 1] + jnp.dot(steps[g - 1], carry, precision=lax.Precision.HIGHEST)
             start = jnp.where(segment == g, carry, start)
-    start = after(start, *late)
+    served = route(whole)
+    start = after(start, *late, served)
     states = (
         jnp.dot(
             before[:, :, :DK].reshape(heads * DK, DK), start, precision=lax.Precision.HIGH
@@ -256,7 +257,7 @@
     back = lax.all_to_all(
         states, AXES, split_axis=0, concat_axis=0, axis_index_groups=groups, tiled=True
     )
-    return back
+    return back, served
 
 
 def finish_kernel(
@@ -604,11 +605,11 @@
     return pieces
 
 
-def to_everyone_early(array, stages):
+def to_everyone_early(array, stages, others):
     pieces = [((0,), array[None])]
     pieces += [send_on(pieces, (0,), stage) for stage in (stages[0], stages[2], stages[3])]
     joined = jnp.concatenate([pieces[0][1], pieces[1][1]], axis=0)
-    joined = after(joined, pieces[2][1], pieces[3][1])
+    joined = after(joined, pieces[2][1], pieces[3][1], *others)
     both = [(pieces[0][0] + pieces[1][0], joined)]
     pieces.append(send_on(both, (0,), stages[1]))
     pieces += [send_on(pieces, (i,), stages[2]) for i in (1, 4)]
@@ -641,27 +642,32 @@
     inner_size = lax.axis_size("inner")
     local_experts = expert_gate.shape[0]
     capacity = max(2, tok_rows * TOP * 8 // (5 * local_experts * devices))
-    early, late = (
-        over_rest(part)[1:] for part in (out_proj[:EARLY_ROWS], out_proj[EARLY_ROWS:])
-    )
-    served_weights = routing(expert_ids, gate_weights, local_experts)
+    late_rows = out_proj[EARLY_ROWS:]
+    early = over_rest(out_proj[:EARLY_ROWS])[1:]
     other_gate, other_up, other_down = (
         flipped(x, inner_size) for x in (expert_gate, expert_up, expert_down)
     )
     maps, mix = local_terms(query_input, key_input, value_input, write_strength, decay_rate)
-    maps = after(maps, *early)
-    others = (other_gate, other_up, other_down)
+    ready = [*early, late_rows, other_gate, other_up, other_down]
+    others = []
     if split_core:
-        core_early = [flipped(piece, inner_size) for piece in [out_proj] + early]
-        others += tuple(core_early)
-    states = entering_states(maps, devices, others, late)
+        core_own = flipped(out_proj, inner_size)
+        core_early = [flipped(piece, inner_size) for piece in early]
+        ready, others = ready + [core_own], core_early
+    maps = after(maps, *ready)
+    late = over_rest(after(late_rows, maps))[1:]
+
+    def route(whole):
+        return routing(after(expert_ids, whole), gate_weights, local_experts)
+
+    states, served_weights = entering_states(maps, devices, others, late, route)
     slots = positions(served_weights, local_experts)
     proj = [(out_proj,)] + list(zip(early, late))
     places = lax.axis_index(REST) ^ jnp.arange(len(proj), dtype=jnp.int32)
     if split_core:
         core = lax.axis_index("core")
-        core_late = [flipped(piece, inner_size) for piece in late]
-        proj += [(core_early[0],)] + list(zip(core_early[1:], core_late))
+        core_late = [flipped(after(piece, served_weights), inner_size) for piece in late]
+        proj += [(core_own,)] + list(zip(core_early, core_late))
         base = places // inner_size * (2 * inner_size) + places % inner_size
         places = jnp.concatenate([base + core * inner_size, base + (1 - core) * inner_size])
     hidden, *normed = finish(
@@ -670,8 +676,9 @@
     bits = slots[0].shape[0].bit_length() - 1
     plain, turned = tuple(range(bits)), tuple((n + bits - 2) % bits for n in range(bits))
     plan = [[(0,)], [(0, 1)], [(0, 1, 2)], [(0, 1, 2), (3,)]]
-    tokens = [(0, *piece) for piece in to_everyone_early(normed[0], plain)]
-    tokens += [(1, *piece) for piece in to_everyone(normed[1], turned, plan)]
+    second = to_everyone(normed[1], turned, plan)
+    first = to_everyone_early(normed[0], plain, [second[2][1]])
+    tokens = [(0, *piece) for piece in first] + [(1, *piece) for piece in second]
     inner, spread = hidden_units(
         tokens, slots, (expert_gate, expert_up), (other_gate, other_up), capacity
     )

time: 315 us -> 310 us (0.984)
  waiting for transfers between devices: 151 us -> 134 us
  starting transfers between devices: 63.7 us -> 76.8 us
    ppermute x31, starting transfers between devices: 39.1 us -> 50.4 us  [stage_flip(): return lax.ppermute(array, AXES, [(i, partner(i)) for i in range(devices)])]
    ppermute x8, waiting for transfers between devices: 20.4 us -> 11.4 us  [flipped(): return lax.ppermute(array, AXES, [(i, i ^ bit) for i in range(devices)])]
    all_to_all x1, waiting for transfers between devices: 8.76 us -> 0.01 us  [routing(): lax.all_to_all(by_chip, SAME_CORE, split_axis=0, concat_axis=0, tiled=True)]
    all_to_all x1, waiting for transfers between devices: 14.8 us -> 18.2 us  [entering_states(): lax.all_to_all(maps, AXES, split_axis=0, concat_axis=0, axis_index_groups...]
    ppermute x31, waiting for transfers between devices: 96.8 us -> 93.5 us  [stage_flip(): return lax.ppermute(array, AXES, [(i, partner(i)) for i in range(devices)])]
    unnamed x80 -> x78, local copies, waits for them, and re-layouts: 16.8 us -> 14.5 us
  transfers between devices with their start and end apart: 43 -> 43, of which waited for: 23 -> 20; matrix products, arithmetic and copies ran while one was open for 6% -> 7% of each run, Pallas kernels for 9% -> 9%
where the time goes in v1:
time: 310 us; the launch traced here: 309 us
  waiting for transfers between devices  134 us (43%)
  starting transfers between devices  76.8 us (25%)
  Pallas kernels  62.1 us (20%)
  local copies, waits for them, and re-layouts  23.1 us (7%)
  other arithmetic  9.31 us (3%)
  matrix products  3.32 us (1%)
    ppermute x31, waiting for transfers between devices, stage_flip(): return lax.ppermute(array, AXES, [(i, partner(i)) for i in range(devices)])  93.5 us
    ppermute x31, starting transfers between devices, stage_flip(): return lax.ppermute(array, AXES, [(i, partner(i)) for i in range(devices)])  50.4 us
    pallas_call x1, Pallas kernels, hidden_units(): pl.pallas_call(functools.partial(hidden_units_kernel, capacity, pieces),...  24.8 us
    all_to_all x1, waiting for transfers between devices, entering_states(): lax.all_to_all(maps, AXES, split_axis=0, concat_axis=0, axis_index_groups...  18.2 us
    pallas_call x4, Pallas kernels, down_strips(): pl.pallas_call(functools.partial(down_kernel, capacity, order), grid=(wid...  16.3 us
    unnamed x78, local copies, waits for them, and re-layouts  14.5 us
    pallas_call x1, Pallas kernels, local_terms(): pl.pallas_call(local_kernel, grid=(groups,), in_specs=[pl.BlockSpec((n, w...  12.4 us
    ppermute x8, waiting for transfers between devices, flipped(): return lax.ppermute(array, AXES, [(i, i ^ bit) for i in range(devices)])  11.4 us
  transfers between devices with their start and end apart: 43, of which 20 were waited for; matrix products, arithmetic and copies ran while one was open for 7% of the time, Pallas kernels for 9%

profile of v1, /device:TPU:0, one launch (start us, length us, event | category | flops | bytes accessed | tf_op | source)
XLA Modules:
  0.0 309.0 jit_solution(11772266363635050655)
XLA Ops:
  2.3 3.0 collective-permute-start
  5.3 2.5 slice.94.refs_2_.refs_0_
  8.4 12.4 %local_terms.1 = (bf16[16,128,384]{2,1,0:T(8,128)(2,1)S(1)}, f32[16,128,256]{2,1,0:T(8,128)S(1)}) custom-call(bf16[128,1024]{1,0:T(8,128)(2,1)S(1)} %copy-done.18, bf16[128,1024]{1,0:T(8,128)(2,1)S(1)} %copy-done.19, bf16[128,2048]{1,0:T(8,128)(2,1)S(1)} %copy-done.11, f32[4,128,4]{2,1,0:T(8,128)S(1)} %bitcast.47, f32[4,4,128]{2,1,0:T(4,128)S(1)} %bitcast.52, ...), custom_call_target="tpu_custom_call" | custom-call | tf_op jit(solution)/shard_map/local_terms/pallas_call | solution.py:151
  24.2 4.9 %all-to-all-start = ((bf16[16,128,384]{2,1,0:T(8,128)(2,1)}), bf16[16,128,384]{2,1,0:T(8,128)(2,1)S(1)}, u32[]{:S(2)}, u32[]{:S(2)}) async-start(bf16[16,128,384]{2,1,0:T(8,128)(2,1)} %after.6.refs_1_), calls=%async_computation | async-start | bytes 3145728 | tf_op jit(solution)/shard_map/all_to_all | solution.py:233
  29.1 2.0 collective-permute-start.7
  31.8 1.9 collective-permute-done.5.refs_0_.refs_4_
  33.7 18.2 %all-to-all-done.maps_ref = bf16[16,128,384]{2,1,0:T(8,128)(2,1)S(1)} async-done(((bf16[16,128,384]{2,1,0:T(8,128)(2,1)}), bf16[16,128,384]{2,1,0:T(8,128)(2,1)S(1)}, u32[]{:S(2)}, u32[]{:S(2)}) %all-to-all-start) | async-done | bytes 1572896 | tf_op jit(solution)/shard_map/all_to_all | solution.py:233
  51.9 3.0 chain.1
  58.5 6.3 %all-to-all-start.1 = ((f32[16,4,128]{2,1,0:T(4,128)}), f32[16,4,128]{2,1,0:T(4,128)S(1)}, u32[]{:S(2)}, u32[]{:S(2)}) async-start(f32[16,4,128]{2,1,0:T(4,128)} %bitcast.10), calls=%async_computation.1 | async-start | bytes 65536 | tf_op jit(solution)/shard_map/all_to_all | solution.py:538
  65.7 4.7 %collective-permute-start.6 = (f32[128,128]{1,0:T(8,128)S(1)}, f32[128,128]{1,0:T(8,128)S(1)}, u32[]{:S(2)}, u32[]{:S(2)}) collective-permute-start(f32[128,128]{1,0:T(8,128)S(1)} %slice.96), channel_id=1, source_target_pairs={{0,16},{1,17},{2,18},{3,19},{4,20},{5,21},{6,22},{7,23},{8,24},{9,... | collective-permute-start | bytes 196616 | tf_op jit(solution)/shard_map/ppermute | solution.py:238
  70.4 9.5 %collective-permute-done.7.refs_1_.refs_2_ = bf16[1280,512]{1,0:T(8,128)(2,1)S(1)} collective-permute-done((bf16[1280,512]{1,0:T(8,128)(2,1)}, bf16[1280,512]{1,0:T(8,128)(2,1)S(1)}, u32[]{:S(2)}, u32[]{:S(2)}) %collective-permute-start.7) | collective-permute-done | bytes 1310752 | tf_op jit(solution)/shard_map/ppermute | solution.py:568
  82.3 2.9 add_convert_fusion.8
  85.3 4.3 %all-to-all-start.2 = ((bf16[16,128,128]{2,1,0:T(8,128)(2,1)}), bf16[16,128,128]{2,1,0:T(8,128)(2,1)S(1)}, u32[]{:S(2)}, u32[]{:S(2)}) async-start(bf16[16,128,128]{2,1,0:T(8,128)(2,1)} %add_convert_fusion.8), calls=%async_computation.2 | async-start | bytes 1048576 | tf_op jit(solution)/shard_map/all_to_all | solution.py:257
  89.7 10.5 %all-to-all-done.2.state_ref = bf16[16,128,128]{2,1,0:T(8,128)(2,1)S(1)} async-done(((bf16[16,128,128]{2,1,0:T(8,128)(2,1)}), bf16[16,128,128]{2,1,0:T(8,128)(2,1)S(1)}, u32[]{:S(2)}, u32[]{:S(2)}) %all-to-all-start.2) | async-done | bytes 524320 | tf_op jit(solution)/shard_map/all_to_all | solution.py:257
  102.3 5.5 %finish.1 = (bf16[128,2048]{1,0:T(8,128)(2,1)S(1)}, bf16[128,1536]{1,0:T(8,128)(2,1)S(1)}, bf16[128,512]{1,0:T(8,128)(2,1)S(1)}) custom-call(s32[4]{0:T(128)S(1)} %pad_add_fusion.place_ref, f32[16,128,256]{2,1,0:T(8,128)} %copy-done.8, bf16[16,128,128]{2,1,0:T(8,128)(2,1)S(1)} %all-to-all-done.2.state_ref, bf16[128,2048]{1,0:T(8,128)(2,1)S(1)} %copy-done.12, ...), custom_call_target="tpu_custom_call" | custom-call | tf_op jit(solution)/shard_map/finish/pallas_call | solution.py:308
  107.8 2.6 collective-permute-start.9
  111.1 1.4 collective-permute-start.10
  112.5 4.4 %collective-permute-done.12.refs_12_ = bf16[1,128,512]{2,1,0:T(8,128)(2,1)S(1)} collective-permute-done((bf16[1,128,512]{2,1,0:T(8,128)(2,1)S(1)}, bf16[1,128,512]{2,1,0:T(8,128)(2,1)S(1)}, u32[]{:S(2)}, u32[]{:S(2)}) %collective-permute-start.12) | collective-permute-done | bytes 131104 | tf_op jit(solution)/shard_map/ppermute | solution.py:590
  117.0 3.7 %collective-permute-done.9.refs_1_ = bf16[1,128,1536]{2,1,0:T(8,128)(2,1)S(1)} collective-permute-done((bf16[1,128,1536]{2,1,0:T(8,128)(2,1)S(1)}, bf16[1,128,1536]{2,1,0:T(8,128)(2,1)S(1)}, u32[]{:S(2)}, u32[]{:S(2)}) %collective-permute-start.9) | collective-permute-done | bytes 393248 | tf_op jit(solution)/shard_map/ppermute | solution.py:590
  121.8 1.6 collective-permute-done.13.refs_3_.refs_13_
  126.8 18.0 %collective-permute-done.14.refs_4_ = bf16[2,128,1536]{2,1,0:T(8,128)(2,1)} collective-permute-done((bf16[2,128,1536]{2,1,0:T(8,128)(2,1)}, bf16[2,128,1536]{2,1,0:T(8,128)(2,1)}, u32[]{:S(2)}, u32[]{:S(2)}) %collective-permute-start.14) | collective-permute-done | bytes 786464 | tf_op jit(solution)/shard_map/ppermute | solution.py:590
  146.8 2.0 pad_maximum_fusion.2
  148.8 1.9 collective-permute-start.21
  155.2 6.3 %collective-permute-done.16.refs_6_ = bf16[2,128,1536]{2,1,0:T(8,128)(2,1)} collective-permute-done((bf16[2,128,1536]{2,1,0:T(8,128)(2,1)}, bf16[2,128,1536]{2,1,0:T(8,128)(2,1)}, u32[]{:S(2)}, u32[]{:S(2)}) %collective-permute-start.16) | collective-permute-done | bytes 786464 | tf_op jit(solution)/shard_map/ppermute | solution.py:590
  162.6 1.4 collective-permute-start.22
  167.4 9.4 %collective-permute-done.22.refs_15_ = bf16[4,128,512]{2,1,0:T(8,128)(2,1)} collective-permute-done((bf16[4,128,512]{2,1,0:T(8,128)(2,1)}, bf16[4,128,512]{2,1,0:T(8,128)(2,1)}, u32[]{:S(2)}, u32[]{:S(2)}) %collective-permute-start.22) | collective-permute-done | bytes 524320 | tf_op jit(solution)/shard_map/ppermute | solution.py:590
  176.7 11.6 %collective-permute-done.23.refs_16_ = bf16[4,128,512]{2,1,0:T(8,128)(2,1)} collective-permute-done((bf16[4,128,512]{2,1,0:T(8,128)(2,1)}, bf16[4,128,512]{2,1,0:T(8,128)(2,1)}, u32[]{:S(2)}, u32[]{:S(2)}) %collective-permute-start.23) | collective-permute-done | bytes 524320 | tf_op jit(solution)/shard_map/ppermute | solution.py:590
  188.4 24.8 %hidden_units.1 = (bf16[4,512,512]{2,1,0:T(8,128)(2,1)}, bf16[16,128,256]{2,1,0:T(8,128)(2,1)}) custom-call(f32[16,4,128]{2,1,0:T(4,128)} %copy.45.slot_row_ref, f32[16,128,4]{2,1,0:T(8,128)} %bitcast_select_fusion.slot_ref, f32[16,128,4]{2,1,0:T(8,128)} %bitcast.55, bf16[2,2048,512]{2,1,0:T(8,128)(2,1)} %own_gate_ref.1, bf16[2,2048,512]{2,1,0:T(8,128)(2,1)} %own_up_ref.1, ...), custom_call_target="tpu_custom_call" | custom-call | tf_op jit(solution)/shard_map/hidden_units/pallas_call | solution.py:437
  213.2 1.6 copy-done
  216.0 3.5 %down_strips.4 = (bf16[8,128,512]{2,1,0:T(8,128)(2,1)S(1)}, bf16[8,128,512]{2,1,0:T(8,128)(2,1)S(1)}) custom-call(bf16[4,512,512]{2,1,0:T(8,128)(2,1)S(1)} %copy-done, bf16[16,128,256]{2,1,0:T(8,128)(2,1)S(1)} %copy-done.1, bf16[2,512,2048]{2,1,0:T(8,128)(2,1)} %own_ref.7, bf16[2,512,2048]{2,1,0:T(8,128)(2,1)} %collective-permute-done.3.refs_5_.other_ref), custom_call_target="tpu_custom_call" | custom-call | tf_op jit(solution)/shard_map/down_strips/pallas_call | solution.py:509
  220.7 4.2 %down_strips.7 = (bf16[8,128,512]{2,1,0:T(8,128)(2,1)S(1)}, bf16[8,128,512]{2,1,0:T(8,128)(2,1)S(1)}) custom-call(bf16[4,512,512]{2,1,0:T(8,128)(2,1)} %get-tuple-element.29.inner_ref, bf16[16,128,256]{2,1,0:T(8,128)(2,1)S(1)} %copy-done.2, bf16[2,512,2048]{2,1,0:T(8,128)(2,1)} %own_ref.7, bf16[2,512,2048]{2,1,0:T(8,128)(2,1)} %collective-permute-done.3.refs_5_.other_ref, ...), custom_call_target="tpu_custom_call" | custom-call | tf_op jit(solution)/shard_map/down_strips/pallas_call | solution.py:509
  225.8 4.2 %down_strips.6 = (bf16[8,128,512]{2,1,0:T(8,128)(2,1)S(1)}, bf16[8,128,512]{2,1,0:T(8,128)(2,1)S(1)}) custom-call(bf16[4,512,512]{2,1,0:T(8,128)(2,1)} %get-tuple-element.29.inner_ref, bf16[16,128,256]{2,1,0:T(8,128)(2,1)S(1)} %copy-done.2, bf16[2,512,2048]{2,1,0:T(8,128)(2,1)} %own_ref.7, bf16[2,512,2048]{2,1,0:T(8,128)(2,1)} %collective-permute-done.3.refs_5_.other_ref, ...), custom_call_target="tpu_custom_call" | custom-call | tf_op jit(solution)/shard_map/down_strips/pallas_call | solution.py:509
  230.4 4.4 %down_strips.5 = (bf16[8,128,512]{2,1,0:T(8,128)(2,1)S(1)}, bf16[8,128,512]{2,1,0:T(8,128)(2,1)S(1)}) custom-call(bf16[4,512,512]{2,1,0:T(8,128)(2,1)} %get-tuple-element.29.inner_ref, bf16[16,128,256]{2,1,0:T(8,128)(2,1)S(1)} %copy-done.2, bf16[2,512,2048]{2,1,0:T(8,128)(2,1)} %own_ref.7, bf16[2,512,2048]{2,1,0:T(8,128)(2,1)} %collective-permute-done.3.refs_5_.other_ref, ...), custom_call_target="tpu_custom_call" | custom-call | tf_op jit(solution)/shard_map/down_strips/pallas_call | solution.py:509
  234.8 1.4 collective-permute-start.28
  236.5 1.6 collective-permute-start.25
  238.1 13.9 %collective-permute-done.36 = bf16[8,128,512]{2,1,0:T(8,128)(2,1)S(1)} collective-permute-done((bf16[8,128,512]{2,1,0:T(8,128)(2,1)S(1)}, bf16[8,128,512]{2,1,0:T(8,128)(2,1)S(1)}, u32[]{:S(2)}, u32[]{:S(2)}) %collective-permute-start.36) | collective-permute-done | bytes 1048608 | tf_op jit(solution)/shard_map/ppermute | solution.py:590
  252.4 1.7 collective-permute-start.37
  254.0 1.8 collective-permute-done.32
  256.2 3.3 %collective-permute-start.33 = (bf16[4,128,512]{2,1,0:T(8,128)(2,1)S(1)}, bf16[4,128,512]{2,1,0:T(8,128)(2,1)S(1)}, u32[]{:S(2)}, u32[]{:S(2)}) collective-permute-start(bf16[4,128,512]{2,1,0:T(8,128)(2,1)S(1)} %slice.141), channel_id=1, source_target_pairs={{0,16},{1,9},{2,18},{3,11},{4,20},{5,13},{6,22},{7,15},{8,24},{9,1... | collective-permute-start | bytes 1572872 | tf_op jit(solution)/shard_map/ppermute | solution.py:590
  259.5 8.6 %collective-permute-done.28 = bf16[8,128,512]{2,1,0:T(8,128)(2,1)S(1)} collective-permute-done((bf16[8,128,512]{2,1,0:T(8,128)(2,1)S(1)}, bf16[8,128,512]{2,1,0:T(8,128)(2,1)S(1)}, u32[]{:S(2)}, u32[]{:S(2)}) %collective-permute-start.28) | collective-permute-done | bytes 1048608 | tf_op jit(solution)/shard_map/ppermute | solution.py:590
  268.4 3.2 %collective-permute-start.29 = (bf16[4,128,512]{2,1,0:T(8,128)(2,1)S(1)}, bf16[4,128,512]{2,1,0:T(8,128)(2,1)S(1)}, u32[]{:S(2)}, u32[]{:S(2)}) collective-permute-start(bf16[4,128,512]{2,1,0:T(8,128)(2,1)S(1)} %slice.135), channel_id=1, source_target_pairs={{0,4},{1,3},{2,6},{3,1},{4,0},{5,7},{6,2},{7,5},{8,12},{9,11},{10,... | collective-permute-start | bytes 1572872 | tf_op jit(solution)/shard_map/ppermute | solution.py:590
  272.1 2.1 collective-permute-start.38
  274.2 9.6 %collective-permute-done.33 = bf16[4,128,512]{2,1,0:T(8,128)(2,1)S(1)} collective-permute-done((bf16[4,128,512]{2,1,0:T(8,128)(2,1)S(1)}, bf16[4,128,512]{2,1,0:T(8,128)(2,1)S(1)}, u32[]{:S(2)}, u32[]{:S(2)}) %collective-permute-start.33) | collective-permute-done | bytes 524320 | tf_op jit(solution)/shard_map/ppermute | solution.py:590
  284.2 3.9 %collective-permute-start.30 = (bf16[2,128,512]{2,1,0:T(8,128)(2,1)S(1)}, bf16[2,128,512]{2,1,0:T(8,128)(2,1)S(1)}, u32[]{:S(2)}, u32[]{:S(2)}) collective-permute-start(bf16[2,128,512]{2,1,0:T(8,128)(2,1)S(1)} %slice.137), channel_id=1, source_target_pairs={{0,8},{1,17},{2,10},{3,19},{4,12},{5,21},{6,14},{7,23},{8,0},{9,25... | collective-permute-start | bytes 786440 | tf_op jit(solution)/shard_map/ppermute | solution.py:590
  288.2 6.7 %collective-permute-start.27 = (bf16[1,128,512]{2,1,0:T(8,128)(2,1)S(1)}, bf16[1,128,512]{2,1,0:T(8,128)(2,1)S(1)}, u32[]{:S(2)}, u32[]{:S(2)}) collective-permute-start(bf16[1,128,512]{2,1,0:T(8,128)(2,1)S(1)} %slice.133), channel_id=1, source_target_pairs={{0,16},{1,9},{2,18},{3,11},{4,20},{5,13},{6,22},{7,15},{8,24},{9,1... | collective-permute-start | bytes 393224 | tf_op jit(solution)/shard_map/ppermute | solution.py:590
  295.0 6.8 %collective-permute-start.39 = (bf16[1,128,512]{2,1,0:T(8,128)(2,1)S(1)}, bf16[1,128,512]{2,1,0:T(8,128)(2,1)S(1)}, u32[]{:S(2)}, u32[]{:S(2)}) collective-permute-start(bf16[1,128,512]{2,1,0:T(8,128)(2,1)S(1)} %slice.151), channel_id=1, source_target_pairs={{0,16},{1,9},{2,18},{3,11},{4,20},{5,13},{6,22},{7,15},{8,24},{9,1... | collective-permute-start | bytes 393224 | tf_op jit(solution)/shard_map/ppermute | solution.py:590
  302.1 2.5 collective-permute-start.31
  304.8 2.1 collective-permute-done.35
  (188 shorter events, 40.3 us)
Async XLA Ops:
  0.0 23.3 %collective-permute-start.1 = (bf16[2,2048,512]{2,1,0:T(8,128)(2,1)}, bf16[2,2048,512]{2,1,0:T(8,128)(2,1)}, u32[]{:S(2)}, u32[]{:S(2)}) collective-permute-start(bf16[2,2048,512]{2,1,0:T(8,128)(2,1)} %own_gate_ref.1), channel_id=1, source_target_pairs={{0,1},{1,0},{2,3},{3,2},{4,5},{5,4},{6,7},{7,6},{8,9},{9,8},{10,11... | collective-permute-start | bytes 12582920 | tf_op jit(solution)/shard_map/ppermute | solution.py:568
  0.5 22.8 %collective-permute-start.2 = (bf16[2,2048,512]{2,1,0:T(8,128)(2,1)}, bf16[2,2048,512]{2,1,0:T(8,128)(2,1)}, u32[]{:S(2)}, u32[]{:S(2)}) collective-permute-start(bf16[2,2048,512]{2,1,0:T(8,128)(2,1)} %own_up_ref.1), channel_id=1, source_target_pairs={{0,1},{1,0},{2,3},{3,2},{4,5},{5,4},{6,7},{7,6},{8,9},{9,8},{10,11... | collective-permute-start | bytes 12582920 | tf_op jit(solution)/shard_map/ppermute | solution.py:568
  0.6 22.7 %collective-permute-start.3 = (bf16[2,512,2048]{2,1,0:T(8,128)(2,1)}, bf16[2,512,2048]{2,1,0:T(8,128)(2,1)}, u32[]{:S(2)}, u32[]{:S(2)}) collective-permute-start(bf16[2,512,2048]{2,1,0:T(8,128)(2,1)} %own_ref.7), channel_id=1, source_target_pairs={{0,1},{1,0},{2,3},{3,2},{4,5},{5,4},{6,7},{7,6},{8,9},{9,8},{10,11... | collective-permute-start | bytes 12582920 | tf_op jit(solution)/shard_map/ppermute | solution.py:568
  1.1 22.2 %collective-permute-start.4 = (bf16[2048,512]{1,0:T(8,128)(2,1)}, bf16[2048,512]{1,0:T(8,128)(2,1)}, u32[]{:S(2)}, u32[]{:S(2)}) collective-permute-start(bf16[2048,512]{1,0:T(8,128)(2,1)} %refs_0_.2), channel_id=1, source_target_pairs={{0,1},{1,0},{2,3},{3,2},{4,5},{5,4},{6,7},{7,6},{8,9},{9,8},{10,11... | collective-permute-start | bytes 6291464 | tf_op jit(solution)/shard_map/ppermute | solution.py:568
  2.3 21.0 %collective-permute-start = (bf16[768,512]{1,0:T(8,128)(2,1)S(1)}, bf16[768,512]{1,0:T(8,128)(2,1)S(1)}, u32[]{:S(2)}, u32[]{:S(2)}) collective-permute-start(bf16[768,512]{1,0:T(8,128)(2,1)S(1)} %slice.93), channel_id=1, source_target_pairs={{0,2},{1,3},{2,0},{3,1},{4,6},{5,7},{6,4},{7,5},{8,10},{9,11},{10,... | collective-permute-start | bytes 2359304 | tf_op jit(solution)/shard_map/ppermute | solution.py:568
  24.2 27.8 %all-to-all-start = ((bf16[16,128,384]{2,1,0:T(8,128)(2,1)}), bf16[16,128,384]{2,1,0:T(8,128)(2,1)S(1)}, u32[]{:S(2)}, u32[]{:S(2)}) async-start(bf16[16,128,384]{2,1,0:T(8,128)(2,1)} %after.6.refs_1_), calls=%async_computation | async-start | bytes 3145728 | tf_op jit(solution)/shard_map/all_to_all | solution.py:233
  29.1 28.8 %copy-start.35 = (f32[128,10]{0,1:T(8,128)S(1)}, f32[128,10]{0,1:T(8,128)}, u32[]{:S(2)}) copy-start(f32[128,10]{0,1:T(8,128)} %param.27) | copy-start | bytes 15364
  29.1 50.8 %collective-permute-start.7 = (bf16[1280,512]{1,0:T(8,128)(2,1)}, bf16[1280,512]{1,0:T(8,128)(2,1)S(1)}, u32[]{:S(2)}, u32[]{:S(2)}) collective-permute-start(bf16[1280,512]{1,0:T(8,128)(2,1)} %after.7), channel_id=1, source_target_pairs={{0,2},{1,3},{2,0},{3,1},{4,6},{5,7},{6,4},{7,5},{8,10},{9,11},{10,... | collective-permute-start | bytes 3932168 | tf_op jit(solution)/shard_map/ppermute | solution.py:568
  31.1 2.6 collective-permute-start.5
  58.5 22.5 %all-to-all-start.1 = ((f32[16,4,128]{2,1,0:T(4,128)}), f32[16,4,128]{2,1,0:T(4,128)S(1)}, u32[]{:S(2)}, u32[]{:S(2)}) async-start(f32[16,4,128]{2,1,0:T(4,128)} %bitcast.10), calls=%async_computation.1 | async-start | bytes 65536 | tf_op jit(solution)/shard_map/all_to_all | solution.py:538
  65.7 16.0 %collective-permute-start.6 = (f32[128,128]{1,0:T(8,128)S(1)}, f32[128,128]{1,0:T(8,128)S(1)}, u32[]{:S(2)}, u32[]{:S(2)}) collective-permute-start(f32[128,128]{1,0:T(8,128)S(1)} %slice.96), channel_id=1, source_target_pairs={{0,16},{1,17},{2,18},{3,19},{4,20},{5,21},{6,22},{7,23},{8,24},{9,... | collective-permute-start | bytes 196616 | tf_op jit(solution)/shard_map/ppermute | solution.py:238
  81.6 18.6 %collective-permute-start.8 = (bf16[1280,512]{1,0:T(8,128)(2,1)}, bf16[1280,512]{1,0:T(8,128)(2,1)}, u32[]{:S(2)}, u32[]{:S(2)}) collective-permute-start(bf16[1280,512]{1,0:T(8,128)(2,1)} %after.10), channel_id=1, source_target_pairs={{0,1},{1,0},{2,3},{3,2},{4,5},{5,4},{6,7},{7,6},{8,9},{9,8},{10,11... | collective-permute-start | bytes 3932168 | tf_op jit(solution)/shard_map/ppermute | solution.py:568
  85.3 14.9 %all-to-all-start.2 = ((bf16[16,128,128]{2,1,0:T(8,128)(2,1)}), bf16[16,128,128]{2,1,0:T(8,128)(2,1)S(1)}, u32[]{:S(2)}, u32[]{:S(2)}) async-start(bf16[16,128,128]{2,1,0:T(8,128)(2,1)} %add_convert_fusion.8), calls=%async_computation.2 | async-start | bytes 1048576 | tf_op jit(solution)/shard_map/all_to_all | solution.py:257
  107.8 39.0 %copy-start.10 = (bf16[128,512]{1,0:T(8,128)(2,1)}, bf16[128,512]{1,0:T(8,128)(2,1)S(1)}, u32[]{:S(2)}) copy-start(bf16[128,512]{1,0:T(8,128)(2,1)S(1)} %get-tuple-element.28) | copy-start | bytes 393220
  107.8 13.0 %collective-permute-start.9 = (bf16[1,128,1536]{2,1,0:T(8,128)(2,1)S(1)}, bf16[1,128,1536]{2,1,0:T(8,128)(2,1)S(1)}, u32[]{:S(2)}, u32[]{:S(2)}) collective-permute-start(bf16[1,128,1536]{2,1,0:T(8,128)(2,1)S(1)} %bitcast.38), channel_id=1, source_target_pairs={{0,16},{1,9},{2,18},{3,11},{4,20},{5,13},{6,22},{7,15},{8,24},{9,1... | collective-permute-start | bytes 1179656 | tf_op jit(solution)/shard_map/ppermute | solution.py:590
  110.5 6.4 %collective-permute-start.12 = (bf16[1,128,512]{2,1,0:T(8,128)(2,1)S(1)}, bf16[1,128,512]{2,1,0:T(8,128)(2,1)S(1)}, u32[]{:S(2)}, u32[]{:S(2)}) collective-permute-start(bf16[1,128,512]{2,1,0:T(8,128)(2,1)S(1)} %bitcast.43), channel_id=1, source_target_pairs={{0,4},{1,3},{2,6},{3,1},{4,0},{5,7},{6,2},{7,5},{8,12},{9,11},{10,... | collective-permute-start | bytes 393224 | tf_op jit(solution)/shard_map/ppermute | solution.py:590
  110.5 12.9 %collective-permute-start.11 = (bf16[1,128,1536]{2,1,0:T(8,128)(2,1)S(1)}, bf16[1,128,1536]{2,1,0:T(8,128)(2,1)S(1)}, u32[]{:S(2)}, u32[]{:S(2)}) collective-permute-start(bf16[1,128,1536]{2,1,0:T(8,128)(2,1)S(1)} %bitcast.39), channel_id=1, source_target_pairs={{0,2},{1,5},{2,0},{3,7},{4,6},{5,1},{6,4},{7,3},{8,10},{9,13},{10,... | collective-permute-start | bytes 1179656 | tf_op jit(solution)/shard_map/ppermute | solution.py:590
  111.1 12.6 %collective-permute-start.10 = (bf16[1,128,1536]{2,1,0:T(8,128)(2,1)S(1)}, bf16[1,128,1536]{2,1,0:T(8,128)(2,1)S(1)}, u32[]{:S(2)}, u32[]{:S(2)}) collective-permute-start(bf16[1,128,1536]{2,1,0:T(8,128)(2,1)S(1)} %bitcast.40), channel_id=1, source_target_pairs={{0,4},{1,3},{2,6},{3,1},{4,0},{5,7},{6,2},{7,5},{8,12},{9,11},{10,... | collective-permute-start | bytes 1179656 | tf_op jit(solution)/shard_map/ppermute | solution.py:590
  116.9 29.9 %copy-start.30 = (bf16[1,128,512]{2,1,0:T(8,128)(2,1)}, bf16[1,128,512]{2,1,0:T(8,128)(2,1)S(1)}, u32[]{:S(2)}) copy-start(bf16[1,128,512]{2,1,0:T(8,128)(2,1)S(1)} %collective-permute-done.12.refs_12_) | copy-start | bytes 393220
  116.9 6.4 %collective-permute-start.13 = (bf16[2,128,512]{2,1,0:T(8,128)(2,1)S(1)}, bf16[2,128,512]{2,1,0:T(8,128)(2,1)S(1)}, u32[]{:S(2)}, u32[]{:S(2)}) collective-permute-start(bf16[2,128,512]{2,1,0:T(8,128)(2,1)S(1)} %pad_maximum_fusion.3), channel_id=1, source_target_pairs={{0,2},{1,5},{2,0},{3,7},{4,6},{5,1},{6,4},{7,3},{8,10},{9,13},{10,... | collective-permute-start | bytes 786440 | tf_op jit(solution)/shard_map/ppermute | solution.py:590
  120.8 30.4 %copy-start.28 = (bf16[1,128,1536]{2,1,0:T(8,128)(2,1)}, bf16[1,128,1536]{2,1,0:T(8,128)(2,1)S(1)}, u32[]{:S(2)}) copy-start(bf16[1,128,1536]{2,1,0:T(8,128)(2,1)S(1)} %collective-permute-done.9.refs_1_) | copy-start | bytes 1179652
  125.0 27.2 %copy-start.25 = (bf16[1,128,1536]{2,1,0:T(8,128)(2,1)S(1)}, bf16[1,128,1536]{2,1,0:T(8,128)(2,1)}, u32[]{:S(2)}) copy-start(bf16[1,128,1536]{2,1,0:T(8,128)(2,1)} %copy-done.24) | copy-start | bytes 1179652
  125.0 19.8 %collective-permute-start.14 = (bf16[2,128,1536]{2,1,0:T(8,128)(2,1)}, bf16[2,128,1536]{2,1,0:T(8,128)(2,1)}, u32[]{:S(2)}, u32[]{:S(2)}) collective-permute-start(bf16[2,128,1536]{2,1,0:T(8,128)(2,1)} %after.11), channel_id=1, source_target_pairs={{0,8},{1,17},{2,10},{3,19},{4,12},{5,21},{6,14},{7,23},{8,0},{9,25... | collective-permute-start | bytes 2359304 | tf_op jit(solution)/shard_map/ppermute | solution.py:590
  125.8 26.3 %collective-permute-start.15 = (bf16[1,128,1536]{2,1,0:T(8,128)(2,1)S(1)}, bf16[1,128,1536]{2,1,0:T(8,128)(2,1)S(1)}, u32[]{:S(2)}, u32[]{:S(2)}) collective-permute-start(bf16[1,128,1536]{2,1,0:T(8,128)(2,1)S(1)} %collective-permute-done.9.refs_1_), channel_id=1, source_target_pairs={{0,4},{1,3},{2,6},{3,1},{4,0},{5,7},{6,2},{7,5},{8,12},{9,11},{10,... | collective-permute-start | bytes 1179656 | tf_op jit(solution)/shard_map/ppermute | solution.py:590
  144.8 16.7 %collective-permute-start.16 = (bf16[2,128,1536]{2,1,0:T(8,128)(2,1)}, bf16[2,128,1536]{2,1,0:T(8,128)(2,1)}, u32[]{:S(2)}, u32[]{:S(2)}) collective-permute-start(bf16[2,128,1536]{2,1,0:T(8,128)(2,1)} %collective-permute-done.14.refs_4_), channel_id=1, source_target_pairs={{0,4},{1,3},{2,6},{3,1},{4,0},{5,7},{6,2},{7,5},{8,12},{9,11},{10,... | collective-permute-start | bytes 2359304 | tf_op jit(solution)/shard_map/ppermute | solution.py:590
  148.8 16.0 %collective-permute-start.21 = (bf16[4,128,512]{2,1,0:T(8,128)(2,1)}, bf16[4,128,512]{2,1,0:T(8,128)(2,1)}, u32[]{:S(2)}, u32[]{:S(2)}) collective-permute-start(bf16[4,128,512]{2,1,0:T(8,128)(2,1)} %pad_maximum_fusion.2), channel_id=1, source_target_pairs={{0,16},{1,9},{2,18},{3,11},{4,20},{5,13},{6,22},{7,15},{8,24},{9,1... | collective-permute-start | bytes 1572872 | tf_op jit(solution)/shard_map/ppermute | solution.py:590
  151.2 11.4 %collective-permute-start.17 = (bf16[1,128,1536]{2,1,0:T(8,128)(2,1)S(1)}, bf16[1,128,1536]{2,1,0:T(8,128)(2,1)}, u32[]{:S(2)}, u32[]{:S(2)}) collective-permute-start(bf16[1,128,1536]{2,1,0:T(8,128)(2,1)S(1)} %collective-permute-done.9.refs_1_), channel_id=1, source_target_pairs={{0,2},{1,5},{2,0},{3,7},{4,6},{5,1},{6,4},{7,3},{8,10},{9,13},{10,... | collective-permute-start | bytes 1179656 | tf_op jit(solution)/shard_map/ppermute | solution.py:590
  153.1 35.2 %collective-permute-start.19 = (bf16[2,128,1536]{2,1,0:T(8,128)(2,1)}, bf16[2,128,1536]{2,1,0:T(8,128)(2,1)}, u32[]{:S(2)}, u32[]{:S(2)}) collective-permute-start(bf16[2,128,1536]{2,1,0:T(8,128)(2,1)} %pad_maximum_fusion.1), channel_id=1, source_target_pairs={{0,2},{1,5},{2,0},{3,7},{4,6},{5,1},{6,4},{7,3},{8,10},{9,13},{10,... | collective-permute-start | bytes 2359304 | tf_op jit(solution)/shard_map/ppermute | solution.py:590
  154.3 34.0 %collective-permute-start.18 = (bf16[2,128,1536]{2,1,0:T(8,128)(2,1)}, bf16[2,128,1536]{2,1,0:T(8,128)(2,1)}, u32[]{:S(2)}, u32[]{:S(2)}) collective-permute-start(bf16[2,128,1536]{2,1,0:T(8,128)(2,1)} %collective-permute-done.14.refs_4_), channel_id=1, source_target_pairs={{0,2},{1,5},{2,0},{3,7},{4,6},{5,1},{6,4},{7,3},{8,10},{9,13},{10,... | collective-permute-start | bytes 2359304 | tf_op jit(solution)/shard_map/ppermute | solution.py:590
  161.5 26.8 %collective-permute-start.20 = (bf16[2,128,1536]{2,1,0:T(8,128)(2,1)}, bf16[2,128,1536]{2,1,0:T(8,128)(2,1)}, u32[]{:S(2)}, u32[]{:S(2)}) collective-permute-start(bf16[2,128,1536]{2,1,0:T(8,128)(2,1)} %collective-permute-done.16.refs_6_), channel_id=1, source_target_pairs={{0,2},{1,5},{2,0},{3,7},{4,6},{5,1},{6,4},{7,3},{8,10},{9,13},{10,... | collective-permute-start | bytes 2359304 | tf_op jit(solution)/shard_map/ppermute | solution.py:590
  162.6 14.1 %collective-permute-start.22 = (bf16[4,128,512]{2,1,0:T(8,128)(2,1)}, bf16[4,128,512]{2,1,0:T(8,128)(2,1)}, u32[]{:S(2)}, u32[]{:S(2)}) collective-permute-start(bf16[4,128,512]{2,1,0:T(8,128)(2,1)} %pad_maximum_fusion.2), channel_id=1, source_target_pairs={{0,8},{1,17},{2,10},{3,19},{4,12},{5,21},{6,14},{7,23},{8,0},{9,25... | collective-permute-start | bytes 1572872 | tf_op jit(solution)/shard_map/ppermute | solution.py:590
  164.8 23.5 %collective-permute-start.23 = (bf16[4,128,512]{2,1,0:T(8,128)(2,1)}, bf16[4,128,512]{2,1,0:T(8,128)(2,1)}, u32[]{:S(2)}, u32[]{:S(2)}) collective-permute-start(bf16[4,128,512]{2,1,0:T(8,128)(2,1)} %collective-permute-done.21.refs_14_), channel_id=1, source_target_pairs={{0,8},{1,17},{2,10},{3,19},{4,12},{5,21},{6,14},{7,23},{8,0},{9,25... | collective-permute-start | bytes 1572872 | tf_op jit(solution)/shard_map/ppermute | solution.py:590
  219.5 16.6 %collective-permute-start.24 = (bf16[8,128,512]{2,1,0:T(8,128)(2,1)S(1)}, bf16[8,128,512]{2,1,0:T(8,128)(2,1)S(1)}, u32[]{:S(2)}, u32[]{:S(2)}) collective-permute-start(bf16[8,128,512]{2,1,0:T(8,128)(2,1)S(1)} %get-tuple-element.32), channel_id=1, source_target_pairs={{0,2},{1,5},{2,0},{3,7},{4,6},{5,1},{6,4},{7,3},{8,10},{9,13},{10,... | collective-permute-start | bytes 3145736 | tf_op jit(solution)/shard_map/ppermute | solution.py:590
  224.9 27.1 %collective-permute-start.36 = (bf16[8,128,512]{2,1,0:T(8,128)(2,1)S(1)}, bf16[8,128,512]{2,1,0:T(8,128)(2,1)S(1)}, u32[]{:S(2)}, u32[]{:S(2)}) collective-permute-start(bf16[8,128,512]{2,1,0:T(8,128)(2,1)S(1)} %get-tuple-element.38), channel_id=1, source_target_pairs={{0,2},{1,5},{2,0},{3,7},{4,6},{5,1},{6,4},{7,3},{8,10},{9,13},{10,... | collective-permute-start | bytes 3145736 | tf_op jit(solution)/shard_map/ppermute | solution.py:590
  230.1 25.8 %collective-permute-start.32 = (bf16[8,128,512]{2,1,0:T(8,128)(2,1)S(1)}, bf16[8,128,512]{2,1,0:T(8,128)(2,1)S(1)}, u32[]{:S(2)}, u32[]{:S(2)}) collective-permute-start(bf16[8,128,512]{2,1,0:T(8,128)(2,1)S(1)} %get-tuple-element.36), channel_id=1, source_target_pairs={{0,8},{1,17},{2,10},{3,19},{4,12},{5,21},{6,14},{7,23},{8,0},{9,25... | collective-permute-start | bytes 3145736 | tf_op jit(solution)/shard_map/ppermute | solution.py:590
  234.8 33.3 %collective-permute-start.28 = (bf16[8,128,512]{2,1,0:T(8,128)(2,1)S(1)}, bf16[8,128,512]{2,1,0:T(8,128)(2,1)S(1)}, u32[]{:S(2)}, u32[]{:S(2)}) collective-permute-start(bf16[8,128,512]{2,1,0:T(8,128)(2,1)S(1)} %get-tuple-element.34), channel_id=1, source_target_pairs={{0,2},{1,5},{2,0},{3,7},{4,6},{5,1},{6,4},{7,3},{8,10},{9,13},{10,... | collective-permute-start | bytes 3145736 | tf_op jit(solution)/shard_map/ppermute | solution.py:590
  236.5 35.2 %collective-permute-start.25 = (bf16[4,128,512]{2,1,0:T(8,128)(2,1)S(1)}, bf16[4,128,512]{2,1,0:T(8,128)(2,1)S(1)}, u32[]{:S(2)}, u32[]{:S(2)}) collective-permute-start(bf16[4,128,512]{2,1,0:T(8,128)(2,1)S(1)} %slice.129), channel_id=1, source_target_pairs={{0,4},{1,3},{2,6},{3,1},{4,0},{5,7},{6,2},{7,5},{8,12},{9,11},{10,... | collective-permute-start | bytes 1572872 | tf_op jit(solution)/shard_map/ppermute | solution.py:590
  252.4 19.6 %collective-permute-start.37 = (bf16[4,128,512]{2,1,0:T(8,128)(2,1)S(1)}, bf16[4,128,512]{2,1,0:T(8,128)(2,1)S(1)}, u32[]{:S(2)}, u32[]{:S(2)}) collective-permute-start(bf16[4,128,512]{2,1,0:T(8,128)(2,1)S(1)} %slice.147), channel_id=1, source_target_pairs={{0,4},{1,3},{2,6},{3,1},{4,0},{5,7},{6,2},{7,5},{8,12},{9,11},{10,... | collective-permute-start | bytes 1572872 | tf_op jit(solution)/shard_map/ppermute | solution.py:590
  256.2 27.6 %collective-permute-start.33 = (bf16[4,128,512]{2,1,0:T(8,128)(2,1)S(1)}, bf16[4,128,512]{2,1,0:T(8,128)(2,1)S(1)}, u32[]{:S(2)}, u32[]{:S(2)}) collective-permute-start(bf16[4,128,512]{2,1,0:T(8,128)(2,1)S(1)} %slice.141), channel_id=1, source_target_pairs={{0,16},{1,9},{2,18},{3,11},{4,20},{5,13},{6,22},{7,15},{8,24},{9,1... | collective-permute-start | bytes 1572872 | tf_op jit(solution)/shard_map/ppermute | solution.py:590
  268.4 15.6 %collective-permute-start.29 = (bf16[4,128,512]{2,1,0:T(8,128)(2,1)S(1)}, bf16[4,128,512]{2,1,0:T(8,128)(2,1)S(1)}, u32[]{:S(2)}, u32[]{:S(2)}) collective-permute-start(bf16[4,128,512]{2,1,0:T(8,128)(2,1)S(1)} %slice.135), channel_id=1, source_target_pairs={{0,4},{1,3},{2,6},{3,1},{4,0},{5,7},{6,2},{7,5},{8,12},{9,11},{10,... | collective-permute-start | bytes 1572872 | tf_op jit(solution)/shard_map/ppermute | solution.py:590
  271.8 16.3 %collective-permute-start.26 = (bf16[2,128,512]{2,1,0:T(8,128)(2,1)S(1)}, bf16[2,128,512]{2,1,0:T(8,128)(2,1)S(1)}, u32[]{:S(2)}, u32[]{:S(2)}) collective-permute-start(bf16[2,128,512]{2,1,0:T(8,128)(2,1)S(1)} %slice.131), channel_id=1, source_target_pairs={{0,8},{1,17},{2,10},{3,19},{4,12},{5,21},{6,14},{7,23},{8,0},{9,25... | collective-permute-start | bytes 786440 | tf_op jit(solution)/shard_map/ppermute | solution.py:590
  272.1 22.8 %collective-permute-start.38 = (bf16[2,128,512]{2,1,0:T(8,128)(2,1)S(1)}, bf16[2,128,512]{2,1,0:T(8,128)(2,1)S(1)}, u32[]{:S(2)}, u32[]{:S(2)}) collective-permute-start(bf16[2,128,512]{2,1,0:T(8,128)(2,1)S(1)} %slice.149), channel_id=1, source_target_pairs={{0,8},{1,17},{2,10},{3,19},{4,12},{5,21},{6,14},{7,23},{8,0},{9,25... | collective-permute-start | bytes 786440 | tf_op jit(solution)/shard_map/ppermute | solution.py:590
  283.9 17.9 %collective-permute-start.34 = (bf16[2,128,512]{2,1,0:T(8,128)(2,1)S(1)}, bf16[2,128,512]{2,1,0:T(8,128)(2,1)S(1)}, u32[]{:S(2)}, u32[]{:S(2)}) collective-permute-start(bf16[2,128,512]{2,1,0:T(8,128)(2,1)S(1)} %slice.143), channel_id=1, source_target_pairs={{0,2},{1,5},{2,0},{3,7},{4,6},{5,1},{6,4},{7,3},{8,10},{9,13},{10,... | collective-permute-start | bytes 786440 | tf_op jit(solution)/shard_map/ppermute | solution.py:590
  284.2 17.8 %collective-permute-start.30 = (bf16[2,128,512]{2,1,0:T(8,128)(2,1)S(1)}, bf16[2,128,512]{2,1,0:T(8,128)(2,1)S(1)}, u32[]{:S(2)}, u32[]{:S(2)}) collective-permute-start(bf16[2,128,512]{2,1,0:T(8,128)(2,1)S(1)} %slice.137), channel_id=1, source_target_pairs={{0,8},{1,17},{2,10},{3,19},{4,12},{5,21},{6,14},{7,23},{8,0},{9,25... | collective-permute-start | bytes 786440 | tf_op jit(solution)/shard_map/ppermute | solution.py:590
  288.2 16.4 %collective-permute-start.27 = (bf16[1,128,512]{2,1,0:T(8,128)(2,1)S(1)}, bf16[1,128,512]{2,1,0:T(8,128)(2,1)S(1)}, u32[]{:S(2)}, u32[]{:S(2)}) collective-permute-start(bf16[1,128,512]{2,1,0:T(8,128)(2,1)S(1)} %slice.133), channel_id=1, source_target_pairs={{0,16},{1,9},{2,18},{3,11},{4,20},{5,13},{6,22},{7,15},{8,24},{9,1... | collective-permute-start | bytes 393224 | tf_op jit(solution)/shard_map/ppermute | solution.py:590
  295.0 9.7 %collective-permute-start.39 = (bf16[1,128,512]{2,1,0:T(8,128)(2,1)S(1)}, bf16[1,128,512]{2,1,0:T(8,128)(2,1)S(1)}, u32[]{:S(2)}, u32[]{:S(2)}) collective-permute-start(bf16[1,128,512]{2,1,0:T(8,128)(2,1)S(1)} %slice.151), channel_id=1, source_target_pairs={{0,16},{1,9},{2,18},{3,11},{4,20},{5,13},{6,22},{7,15},{8,24},{9,1... | collective-permute-start | bytes 393224 | tf_op jit(solution)/shard_map/ppermute | solution.py:590
  301.9 5.0 %collective-permute-start.35 = (bf16[1,128,512]{2,1,0:T(8,128)(2,1)S(1)}, bf16[1,128,512]{2,1,0:T(8,128)(2,1)S(1)}, u32[]{:S(2)}, u32[]{:S(2)}) collective-permute-start(bf16[1,128,512]{2,1,0:T(8,128)(2,1)S(1)} %slice.145), channel_id=1, source_target_pairs={{0,4},{1,3},{2,6},{3,1},{4,0},{5,7},{6,2},{7,5},{8,12},{9,11},{10,... | collective-permute-start | bytes 393224 | tf_op jit(solution)/shard_map/ppermute | solution.py:590
  302.1 6.0 %collective-permute-start.31 = (bf16[1,128,512]{2,1,0:T(8,128)(2,1)S(1)}, bf16[1,128,512]{2,1,0:T(8,128)(2,1)S(1)}, u32[]{:S(2)}, u32[]{:S(2)}) collective-permute-start(bf16[1,128,512]{2,1,0:T(8,128)(2,1)S(1)} %slice.139), channel_id=1, source_target_pairs={{0,16},{1,9},{2,18},{3,11},{4,20},{5,13},{6,22},{7,15},{8,24},{9,1... | collective-permute-start | bytes 393224 | tf_op jit(solution)/shard_map/ppermute | solution.py:590
  (33 other events, 233.0 us)

commit v2 on v1

--- a/solution.py
+++ b/solution.py
@@ -655,7 +655,7 @@
         core_early = [flipped(piece, inner_size) for piece in early]
         ready, others = ready + [core_own], core_early
     maps = after(maps, *ready)
-    late = over_rest(after(late_rows, maps))[1:]
+    late = over_rest(after(late_rows, *early))[1:]
 
     def route(whole):
         return routing(after(expert_ids, whole), gate_weights, local_experts)
@@ -683,7 +683,7 @@
         tokens, slots, (expert_gate, expert_up), (other_gate, other_up), capacity
     )
     sums, start, before = [], 0, ()
-    for width, stages in ((512, plain), (512, plain), (512, turned), (512, plain)):
+    for width, stages in ((512, plain), (512, plain), (512, plain), (512, turned)):
         keep, send = down_strips(
             inner, spread, expert_down, other_down, capacity, stages[::-1], start, width, before
         )

time: 310 us -> 306 us (0.987)
  starting transfers between devices: 76.8 us -> 68.7 us
    ppermute x31, starting transfers between devices: 50.4 us -> 42.3 us  [stage_flip(): return lax.ppermute(array, AXES, [(i, partner(i)) for i in range(devices)])]
    ppermute x31, waiting for transfers between devices: 93.5 us -> 97.9 us  [stage_flip(): return lax.ppermute(array, AXES, [(i, partner(i)) for i in range(devices)])]
    unnamed x78 -> x80, local copies, waits for them, and re-layouts: 14.5 us -> 14.6 us
  transfers between devices with their start and end apart: 43 -> 43, of which waited for: 20 -> 21; matrix products, arithmetic and copies ran while one was open for 7% -> 7% of each run, Pallas kernels for 9% -> 10%
where the time goes in v2:
time: 306 us; the launch traced here: 305 us
  waiting for transfers between devices  137 us (45%)
  starting transfers between devices  68.7 us (22%)
  Pallas kernels  63.3 us (21%)
  local copies, waits for them, and re-layouts  23.3 us (8%)
  other arithmetic  9.28 us (3%)
  matrix products  3.32 us (1%)
    ppermute x31, waiting for transfers between devices, stage_flip(): return lax.ppermute(array, AXES, [(i, partner(i)) for i in range(devices)])  97.9 us
    ppermute x31, starting transfers between devices, stage_flip(): return lax.ppermute(array, AXES, [(i, partner(i)) for i in range(devices)])  42.3 us
    pallas_call x1, Pallas kernels, hidden_units(): pl.pallas_call(functools.partial(hidden_units_kernel, capacity, pieces),...  24.9 us
    all_to_all x1, waiting for transfers between devices, entering_states(): lax.all_to_all(maps, AXES, split_axis=0, concat_axis=0, axis_index_groups...  18.7 us
    pallas_call x4, Pallas kernels, down_strips(): pl.pallas_call(functools.partial(down_kernel, capacity, order), grid=(wid...  16.3 us
    unnamed x80, local copies, waits for them, and re-layouts  14.6 us
    pallas_call x1, Pallas kernels, local_terms(): pl.pallas_call(local_kernel, grid=(groups,), in_specs=[pl.BlockSpec((n, w...  12.4 us
    all_to_all x1, waiting for transfers between devices, entering_states(): lax.all_to_all(states, AXES, split_axis=0, concat_axis=0, axis_index_grou...  10.5 us
  transfers between devices with their start and end apart: 43, of which 21 were waited for; matrix products, arithmetic and copies ran while one was open for 7% of the time, Pallas kernels for 10%

profile of v2, /device:TPU:0, one launch (start us, length us, event | category | flops | bytes accessed | tf_op | source)
XLA Modules:
  0.0 305.1 jit_solution(15057779571470525040)
XLA Ops:
  2.3 3.0 collective-permute-start
  5.3 2.5 slice.94.refs_2_.refs_0_
  8.4 12.4 %local_terms.1 = (bf16[16,128,384]{2,1,0:T(8,128)(2,1)S(1)}, f32[16,128,256]{2,1,0:T(8,128)S(1)}) custom-call(bf16[128,1024]{1,0:T(8,128)(2,1)S(1)} %copy-done.18, bf16[128,1024]{1,0:T(8,128)(2,1)S(1)} %copy-done.19, bf16[128,2048]{1,0:T(8,128)(2,1)S(1)} %copy-done.11, f32[4,128,4]{2,1,0:T(8,128)S(1)} %bitcast.47, f32[4,4,128]{2,1,0:T(4,128)S(1)} %bitcast.52, ...), custom_call_target="tpu_custom_call" | custom-call | tf_op jit(solution)/shard_map/local_terms/pallas_call | solution.py:151
  24.2 4.9 %all-to-all-start = ((bf16[16,128,384]{2,1,0:T(8,128)(2,1)}), bf16[16,128,384]{2,1,0:T(8,128)(2,1)}, u32[]{:S(2)}, u32[]{:S(2)}) async-start(bf16[16,128,384]{2,1,0:T(8,128)(2,1)} %after.6), calls=%async_computation | async-start | bytes 3145728 | tf_op jit(solution)/shard_map/all_to_all | solution.py:233
  29.2 1.9 collective-permute-start.7
  31.9 1.5 collective-permute-done.5.refs_0_.refs_4_
  33.4 18.7 %all-to-all-done.maps_ref = bf16[16,128,384]{2,1,0:T(8,128)(2,1)} async-done(((bf16[16,128,384]{2,1,0:T(8,128)(2,1)}), bf16[16,128,384]{2,1,0:T(8,128)(2,1)}, u32[]{:S(2)}, u32[]{:S(2)}) %all-to-all-start) | async-done | bytes 1572896 | tf_op jit(solution)/shard_map/all_to_all | solution.py:233
  52.1 4.4 %chain.1 = (f32[16,128,256]{2,1,0:T(8,128)S(1)}, f32[128,256]{1,0:T(8,128)S(1)}) custom-call(bf16[16,128,384]{2,1,0:T(8,128)(2,1)} %all-to-all-done.maps_ref, bf16[768,512]{1,0:T(8,128)(2,1)S(1)} %collective-permute-done.5.refs_0_.refs_4_), custom_call_target="tpu_custom_call" | custom-call | tf_op jit(solution)/shard_map/chain/pallas_call | solution.py:200
  60.1 6.3 %all-to-all-start.1 = ((f32[16,4,128]{2,1,0:T(4,128)}), f32[16,4,128]{2,1,0:T(4,128)S(1)}, u32[]{:S(2)}, u32[]{:S(2)}) async-start(f32[16,4,128]{2,1,0:T(4,128)} %bitcast.10), calls=%async_computation.1 | async-start | bytes 65536 | tf_op jit(solution)/shard_map/all_to_all | solution.py:538
  67.2 4.7 %collective-permute-start.6 = (f32[128,128]{1,0:T(8,128)S(1)}, f32[128,128]{1,0:T(8,128)S(1)}, u32[]{:S(2)}, u32[]{:S(2)}) collective-permute-start(f32[128,128]{1,0:T(8,128)S(1)} %slice.96), channel_id=1, source_target_pairs={{0,16},{1,17},{2,18},{3,19},{4,20},{5,21},{6,22},{7,23},{8,24},{9,... | collective-permute-start | bytes 196616 | tf_op jit(solution)/shard_map/ppermute | solution.py:238
  71.9 8.0 %collective-permute-done.7.refs_1_.refs_2_ = bf16[1280,512]{1,0:T(8,128)(2,1)S(1)} collective-permute-done((bf16[1280,512]{1,0:T(8,128)(2,1)}, bf16[1280,512]{1,0:T(8,128)(2,1)S(1)}, u32[]{:S(2)}, u32[]{:S(2)}) %collective-permute-start.7) | collective-permute-done | bytes 1310752 | tf_op jit(solution)/shard_map/ppermute | solution.py:568
  82.4 2.9 add_convert_fusion.8
  85.3 4.3 %all-to-all-start.2 = ((bf16[16,128,128]{2,1,0:T(8,128)(2,1)}), bf16[16,128,128]{2,1,0:T(8,128)(2,1)S(1)}, u32[]{:S(2)}, u32[]{:S(2)}) async-start(bf16[16,128,128]{2,1,0:T(8,128)(2,1)} %add_convert_fusion.8), calls=%async_computation.2 | async-start | bytes 1048576 | tf_op jit(solution)/shard_map/all_to_all | solution.py:257
  89.7 10.5 %all-to-all-done.2.state_ref = bf16[16,128,128]{2,1,0:T(8,128)(2,1)S(1)} async-done(((bf16[16,128,128]{2,1,0:T(8,128)(2,1)}), bf16[16,128,128]{2,1,0:T(8,128)(2,1)S(1)}, u32[]{:S(2)}, u32[]{:S(2)}) %all-to-all-start.2) | async-done | bytes 524320 | tf_op jit(solution)/shard_map/all_to_all | solution.py:257
  102.3 5.3 %finish.1 = (bf16[128,2048]{1,0:T(8,128)(2,1)S(1)}, bf16[128,1536]{1,0:T(8,128)(2,1)S(1)}, bf16[128,512]{1,0:T(8,128)(2,1)S(1)}) custom-call(s32[4]{0:T(128)S(1)} %pad_add_fusion.place_ref, f32[16,128,256]{2,1,0:T(8,128)} %copy-done.8, bf16[16,128,128]{2,1,0:T(8,128)(2,1)S(1)} %all-to-all-done.2.state_ref, bf16[128,2048]{1,0:T(8,128)(2,1)S(1)} %copy-done.12, ...), custom_call_target="tpu_custom_call" | custom-call | tf_op jit(solution)/shard_map/finish/pallas_call | solution.py:308
  107.6 2.7 collective-permute-start.9
  112.3 4.4 %collective-permute-done.12.refs_12_ = bf16[1,128,512]{2,1,0:T(8,128)(2,1)S(1)} collective-permute-done((bf16[1,128,512]{2,1,0:T(8,128)(2,1)S(1)}, bf16[1,128,512]{2,1,0:T(8,128)(2,1)S(1)}, u32[]{:S(2)}, u32[]{:S(2)}) %collective-permute-start.12) | collective-permute-done | bytes 131104 | tf_op jit(solution)/shard_map/ppermute | solution.py:590
  116.9 3.7 %collective-permute-done.9.refs_1_ = bf16[1,128,1536]{2,1,0:T(8,128)(2,1)S(1)} collective-permute-done((bf16[1,128,1536]{2,1,0:T(8,128)(2,1)S(1)}, bf16[1,128,1536]{2,1,0:T(8,128)(2,1)S(1)}, u32[]{:S(2)}, u32[]{:S(2)}) %collective-permute-start.9) | collective-permute-done | bytes 393248 | tf_op jit(solution)/shard_map/ppermute | solution.py:590
  121.6 1.6 collective-permute-done.13.refs_3_.refs_13_
  126.6 18.1 %collective-permute-done.14.refs_4_ = bf16[2,128,1536]{2,1,0:T(8,128)(2,1)} collective-permute-done((bf16[2,128,1536]{2,1,0:T(8,128)(2,1)}, bf16[2,128,1536]{2,1,0:T(8,128)(2,1)}, u32[]{:S(2)}, u32[]{:S(2)}) %collective-permute-start.14) | collective-permute-done | bytes 786464 | tf_op jit(solution)/shard_map/ppermute | solution.py:590
  146.7 2.0 pad_maximum_fusion.2
  148.7 1.9 collective-permute-start.21
  155.0 6.4 %collective-permute-done.16.refs_6_ = bf16[2,128,1536]{2,1,0:T(8,128)(2,1)} collective-permute-done((bf16[2,128,1536]{2,1,0:T(8,128)(2,1)}, bf16[2,128,1536]{2,1,0:T(8,128)(2,1)}, u32[]{:S(2)}, u32[]{:S(2)}) %collective-permute-start.16) | collective-permute-done | bytes 786464 | tf_op jit(solution)/shard_map/ppermute | solution.py:590
  162.5 1.5 collective-permute-start.22
  167.2 9.5 %collective-permute-done.22.refs_15_ = bf16[4,128,512]{2,1,0:T(8,128)(2,1)} collective-permute-done((bf16[4,128,512]{2,1,0:T(8,128)(2,1)}, bf16[4,128,512]{2,1,0:T(8,128)(2,1)}, u32[]{:S(2)}, u32[]{:S(2)}) %collective-permute-start.22) | collective-permute-done | bytes 524320 | tf_op jit(solution)/shard_map/ppermute | solution.py:590
  176.7 11.5 %collective-permute-done.23.refs_16_ = bf16[4,128,512]{2,1,0:T(8,128)(2,1)} collective-permute-done((bf16[4,128,512]{2,1,0:T(8,128)(2,1)}, bf16[4,128,512]{2,1,0:T(8,128)(2,1)}, u32[]{:S(2)}, u32[]{:S(2)}) %collective-permute-start.23) | collective-permute-done | bytes 524320 | tf_op jit(solution)/shard_map/ppermute | solution.py:590
  188.2 24.9 %hidden_units.1 = (bf16[4,512,512]{2,1,0:T(8,128)(2,1)}, bf16[16,128,256]{2,1,0:T(8,128)(2,1)}) custom-call(f32[16,4,128]{2,1,0:T(4,128)} %copy.45.slot_row_ref, f32[16,128,4]{2,1,0:T(8,128)} %bitcast_select_fusion.slot_ref, f32[16,128,4]{2,1,0:T(8,128)} %bitcast.55, bf16[2,2048,512]{2,1,0:T(8,128)(2,1)} %own_gate_ref.1, bf16[2,2048,512]{2,1,0:T(8,128)(2,1)} %own_up_ref.1, ...), custom_call_target="tpu_custom_call" | custom-call | tf_op jit(solution)/shard_map/hidden_units/pallas_call | solution.py:437
  213.1 1.6 copy-done
  215.9 3.5 %down_strips.4 = (bf16[8,128,512]{2,1,0:T(8,128)(2,1)S(1)}, bf16[8,128,512]{2,1,0:T(8,128)(2,1)S(1)}) custom-call(bf16[4,512,512]{2,1,0:T(8,128)(2,1)S(1)} %copy-done, bf16[16,128,256]{2,1,0:T(8,128)(2,1)S(1)} %copy-done.1, bf16[2,512,2048]{2,1,0:T(8,128)(2,1)} %own_ref.7, bf16[2,512,2048]{2,1,0:T(8,128)(2,1)} %collective-permute-done.3.refs_5_.other_ref), custom_call_target="tpu_custom_call" | custom-call | tf_op jit(solution)/shard_map/down_strips/pallas_call | solution.py:509
  220.6 4.2 %down_strips.7 = (bf16[8,128,512]{2,1,0:T(8,128)(2,1)S(1)}, bf16[8,128,512]{2,1,0:T(8,128)(2,1)S(1)}) custom-call(bf16[4,512,512]{2,1,0:T(8,128)(2,1)} %get-tuple-element.29.inner_ref, bf16[16,128,256]{2,1,0:T(8,128)(2,1)S(1)} %copy-done.2, bf16[2,512,2048]{2,1,0:T(8,128)(2,1)} %own_ref.7, bf16[2,512,2048]{2,1,0:T(8,128)(2,1)} %collective-permute-done.3.refs_5_.other_ref, ...), custom_call_target="tpu_custom_call" | custom-call | tf_op jit(solution)/shard_map/down_strips/pallas_call | solution.py:509
  225.3 4.2 %down_strips.6 = (bf16[8,128,512]{2,1,0:T(8,128)(2,1)S(1)}, bf16[8,128,512]{2,1,0:T(8,128)(2,1)S(1)}) custom-call(bf16[4,512,512]{2,1,0:T(8,128)(2,1)} %get-tuple-element.29.inner_ref, bf16[16,128,256]{2,1,0:T(8,128)(2,1)S(1)} %copy-done.2, bf16[2,512,2048]{2,1,0:T(8,128)(2,1)} %own_ref.7, bf16[2,512,2048]{2,1,0:T(8,128)(2,1)} %collective-permute-done.3.refs_5_.other_ref, ...), custom_call_target="tpu_custom_call" | custom-call | tf_op jit(solution)/shard_map/down_strips/pallas_call | solution.py:509
  230.3 4.4 %down_strips.5 = (bf16[8,128,512]{2,1,0:T(8,128)(2,1)S(1)}, bf16[8,128,512]{2,1,0:T(8,128)(2,1)S(1)}) custom-call(bf16[4,512,512]{2,1,0:T(8,128)(2,1)} %get-tuple-element.29.inner_ref, bf16[16,128,256]{2,1,0:T(8,128)(2,1)S(1)} %copy-done.2, bf16[2,512,2048]{2,1,0:T(8,128)(2,1)} %own_ref.7, bf16[2,512,2048]{2,1,0:T(8,128)(2,1)} %collective-permute-done.3.refs_5_.other_ref, ...), custom_call_target="tpu_custom_call" | custom-call | tf_op jit(solution)/shard_map/down_strips/pallas_call | solution.py:509
  236.4 1.6 collective-permute-start.25
  238.0 12.3 %collective-permute-done.36 = bf16[8,128,512]{2,1,0:T(8,128)(2,1)S(1)} collective-permute-done((bf16[8,128,512]{2,1,0:T(8,128)(2,1)S(1)}, bf16[8,128,512]{2,1,0:T(8,128)(2,1)S(1)}, u32[]{:S(2)}, u32[]{:S(2)}) %collective-permute-start.36) | collective-permute-done | bytes 1048608 | tf_op jit(solution)/shard_map/ppermute | solution.py:590
  250.7 1.8 collective-permute-start.37
  254.2 14.1 %collective-permute-done.28 = bf16[8,128,512]{2,1,0:T(8,128)(2,1)S(1)} collective-permute-done((bf16[8,128,512]{2,1,0:T(8,128)(2,1)S(1)}, bf16[8,128,512]{2,1,0:T(8,128)(2,1)S(1)}, u32[]{:S(2)}, u32[]{:S(2)}) %collective-permute-start.28) | collective-permute-done | bytes 1048608 | tf_op jit(solution)/shard_map/ppermute | solution.py:590
  268.6 2.0 collective-permute-start.29
  270.8 2.3 collective-permute-start.26
  273.8 2.1 collective-permute-start.34
  275.9 2.4 collective-permute-done.29
  278.4 2.2 collective-permute-start.30
  280.6 1.8 collective-permute-done.26
  282.5 7.3 %collective-permute-start.27 = (bf16[1,128,512]{2,1,0:T(8,128)(2,1)S(1)}, bf16[1,128,512]{2,1,0:T(8,128)(2,1)S(1)}, u32[]{:S(2)}, u32[]{:S(2)}) collective-permute-start(bf16[1,128,512]{2,1,0:T(8,128)(2,1)S(1)} %slice.133), channel_id=1, source_target_pairs={{0,16},{1,9},{2,18},{3,11},{4,20},{5,13},{6,22},{7,15},{8,24},{9,1... | collective-permute-start | bytes 393224 | tf_op jit(solution)/shard_map/ppermute | solution.py:590
  290.0 3.0 collective-permute-done.34
  294.3 2.4 collective-permute-done.30
  296.8 1.7 collective-permute-start.31
  298.6 1.8 collective-permute-done.35
  300.4 3.7 %collective-permute-done.31 = bf16[1,128,512]{2,1,0:T(8,128)(2,1)S(1)} collective-permute-done((bf16[1,128,512]{2,1,0:T(8,128)(2,1)S(1)}, bf16[1,128,512]{2,1,0:T(8,128)(2,1)S(1)}, u32[]{:S(2)}, u32[]{:S(2)}) %collective-permute-start.31) | collective-permute-done | bytes 131104 | tf_op jit(solution)/shard_map/ppermute | solution.py:590
  (190 shorter events, 44.4 us)
Async XLA Ops:
  0.0 23.3 %collective-permute-start.1 = (bf16[2,2048,512]{2,1,0:T(8,128)(2,1)}, bf16[2,2048,512]{2,1,0:T(8,128)(2,1)}, u32[]{:S(2)}, u32[]{:S(2)}) collective-permute-start(bf16[2,2048,512]{2,1,0:T(8,128)(2,1)} %own_gate_ref.1), channel_id=1, source_target_pairs={{0,1},{1,0},{2,3},{3,2},{4,5},{5,4},{6,7},{7,6},{8,9},{9,8},{10,11... | collective-permute-start | bytes 12582920 | tf_op jit(solution)/shard_map/ppermute | solution.py:568
  0.5 22.8 %collective-permute-start.2 = (bf16[2,2048,512]{2,1,0:T(8,128)(2,1)}, bf16[2,2048,512]{2,1,0:T(8,128)(2,1)}, u32[]{:S(2)}, u32[]{:S(2)}) collective-permute-start(bf16[2,2048,512]{2,1,0:T(8,128)(2,1)} %own_up_ref.1), channel_id=1, source_target_pairs={{0,1},{1,0},{2,3},{3,2},{4,5},{5,4},{6,7},{7,6},{8,9},{9,8},{10,11... | collective-permute-start | bytes 12582920 | tf_op jit(solution)/shard_map/ppermute | solution.py:568
  0.6 22.7 %collective-permute-start.3 = (bf16[2,512,2048]{2,1,0:T(8,128)(2,1)}, bf16[2,512,2048]{2,1,0:T(8,128)(2,1)}, u32[]{:S(2)}, u32[]{:S(2)}) collective-permute-start(bf16[2,512,2048]{2,1,0:T(8,128)(2,1)} %own_ref.7), channel_id=1, source_target_pairs={{0,1},{1,0},{2,3},{3,2},{4,5},{5,4},{6,7},{7,6},{8,9},{9,8},{10,11... | collective-permute-start | bytes 12582920 | tf_op jit(solution)/shard_map/ppermute | solution.py:568
  1.1 22.3 %collective-permute-start.4 = (bf16[2048,512]{1,0:T(8,128)(2,1)}, bf16[2048,512]{1,0:T(8,128)(2,1)}, u32[]{:S(2)}, u32[]{:S(2)}) collective-permute-start(bf16[2048,512]{1,0:T(8,128)(2,1)} %refs_0_.2), channel_id=1, source_target_pairs={{0,1},{1,0},{2,3},{3,2},{4,5},{5,4},{6,7},{7,6},{8,9},{9,8},{10,11... | collective-permute-start | bytes 6291464 | tf_op jit(solution)/shard_map/ppermute | solution.py:568
  2.3 21.0 %collective-permute-start = (bf16[768,512]{1,0:T(8,128)(2,1)S(1)}, bf16[768,512]{1,0:T(8,128)(2,1)S(1)}, u32[]{:S(2)}, u32[]{:S(2)}) collective-permute-start(bf16[768,512]{1,0:T(8,128)(2,1)S(1)} %slice.93), channel_id=1, source_target_pairs={{0,2},{1,3},{2,0},{3,1},{4,6},{5,7},{6,4},{7,5},{8,10},{9,11},{10,... | collective-permute-start | bytes 2359304 | tf_op jit(solution)/shard_map/ppermute | solution.py:568
  24.2 27.9 %all-to-all-start = ((bf16[16,128,384]{2,1,0:T(8,128)(2,1)}), bf16[16,128,384]{2,1,0:T(8,128)(2,1)}, u32[]{:S(2)}, u32[]{:S(2)}) async-start(bf16[16,128,384]{2,1,0:T(8,128)(2,1)} %after.6), calls=%async_computation | async-start | bytes 3145728 | tf_op jit(solution)/shard_map/all_to_all | solution.py:233
  29.2 30.2 %copy-start.36 = (f32[128,10]{0,1:T(8,128)S(1)}, f32[128,10]{0,1:T(8,128)}, u32[]{:S(2)}) copy-start(f32[128,10]{0,1:T(8,128)} %param.27) | copy-start | bytes 15364
  29.2 50.7 %collective-permute-start.7 = (bf16[1280,512]{1,0:T(8,128)(2,1)}, bf16[1280,512]{1,0:T(8,128)(2,1)S(1)}, u32[]{:S(2)}, u32[]{:S(2)}) collective-permute-start(bf16[1280,512]{1,0:T(8,128)(2,1)} %after.7), channel_id=1, source_target_pairs={{0,2},{1,3},{2,0},{3,1},{4,6},{5,7},{6,4},{7,5},{8,10},{9,11},{10,... | collective-permute-start | bytes 3932168 | tf_op jit(solution)/shard_map/ppermute | solution.py:568
  31.1 2.3 collective-permute-start.5
  60.1 21.0 %all-to-all-start.1 = ((f32[16,4,128]{2,1,0:T(4,128)}), f32[16,4,128]{2,1,0:T(4,128)S(1)}, u32[]{:S(2)}, u32[]{:S(2)}) async-start(f32[16,4,128]{2,1,0:T(4,128)} %bitcast.10), calls=%async_computation.1 | async-start | bytes 65536 | tf_op jit(solution)/shard_map/all_to_all | solution.py:538
  67.2 14.5 %collective-permute-start.6 = (f32[128,128]{1,0:T(8,128)S(1)}, f32[128,128]{1,0:T(8,128)S(1)}, u32[]{:S(2)}, u32[]{:S(2)}) collective-permute-start(f32[128,128]{1,0:T(8,128)S(1)} %slice.96), channel_id=1, source_target_pairs={{0,16},{1,17},{2,18},{3,19},{4,20},{5,21},{6,22},{7,23},{8,24},{9,... | collective-permute-start | bytes 196616 | tf_op jit(solution)/shard_map/ppermute | solution.py:238
  81.6 18.6 %collective-permute-start.8 = (bf16[1280,512]{1,0:T(8,128)(2,1)}, bf16[1280,512]{1,0:T(8,128)(2,1)}, u32[]{:S(2)}, u32[]{:S(2)}) collective-permute-start(bf16[1280,512]{1,0:T(8,128)(2,1)} %after.10), channel_id=1, source_target_pairs={{0,1},{1,0},{2,3},{3,2},{4,5},{5,4},{6,7},{7,6},{8,9},{9,8},{10,11... | collective-permute-start | bytes 3932168 | tf_op jit(solution)/shard_map/ppermute | solution.py:568
  85.3 14.9 %all-to-all-start.2 = ((bf16[16,128,128]{2,1,0:T(8,128)(2,1)}), bf16[16,128,128]{2,1,0:T(8,128)(2,1)S(1)}, u32[]{:S(2)}, u32[]{:S(2)}) async-start(bf16[16,128,128]{2,1,0:T(8,128)(2,1)} %add_convert_fusion.8), calls=%async_computation.2 | async-start | bytes 1048576 | tf_op jit(solution)/shard_map/all_to_all | solution.py:257
  107.6 39.0 %copy-start.10 = (bf16[128,512]{1,0:T(8,128)(2,1)}, bf16[128,512]{1,0:T(8,128)(2,1)S(1)}, u32[]{:S(2)}) copy-start(bf16[128,512]{1,0:T(8,128)(2,1)S(1)} %get-tuple-element.28) | copy-start | bytes 393220
  107.6 13.0 %collective-permute-start.9 = (bf16[1,128,1536]{2,1,0:T(8,128)(2,1)S(1)}, bf16[1,128,1536]{2,1,0:T(8,128)(2,1)S(1)}, u32[]{:S(2)}, u32[]{:S(2)}) collective-permute-start(bf16[1,128,1536]{2,1,0:T(8,128)(2,1)S(1)} %bitcast.38), channel_id=1, source_target_pairs={{0,16},{1,9},{2,18},{3,11},{4,20},{5,13},{6,22},{7,15},{8,24},{9,1... | collective-permute-start | bytes 1179656 | tf_op jit(solution)/shard_map/ppermute | solution.py:590
  110.3 6.4 %collective-permute-start.12 = (bf16[1,128,512]{2,1,0:T(8,128)(2,1)S(1)}, bf16[1,128,512]{2,1,0:T(8,128)(2,1)S(1)}, u32[]{:S(2)}, u32[]{:S(2)}) collective-permute-start(bf16[1,128,512]{2,1,0:T(8,128)(2,1)S(1)} %bitcast.43), channel_id=1, source_target_pairs={{0,4},{1,3},{2,6},{3,1},{4,0},{5,7},{6,2},{7,5},{8,12},{9,11},{10,... | collective-permute-start | bytes 393224 | tf_op jit(solution)/shard_map/ppermute | solution.py:590
  110.3 12.9 %collective-permute-start.11 = (bf16[1,128,1536]{2,1,0:T(8,128)(2,1)S(1)}, bf16[1,128,1536]{2,1,0:T(8,128)(2,1)S(1)}, u32[]{:S(2)}, u32[]{:S(2)}) collective-permute-start(bf16[1,128,1536]{2,1,0:T(8,128)(2,1)S(1)} %bitcast.39), channel_id=1, source_target_pairs={{0,2},{1,5},{2,0},{3,7},{4,6},{5,1},{6,4},{7,3},{8,10},{9,13},{10,... | collective-permute-start | bytes 1179656 | tf_op jit(solution)/shard_map/ppermute | solution.py:590
  110.9 12.6 %collective-permute-start.10 = (bf16[1,128,1536]{2,1,0:T(8,128)(2,1)S(1)}, bf16[1,128,1536]{2,1,0:T(8,128)(2,1)S(1)}, u32[]{:S(2)}, u32[]{:S(2)}) collective-permute-start(bf16[1,128,1536]{2,1,0:T(8,128)(2,1)S(1)} %bitcast.40), channel_id=1, source_target_pairs={{0,4},{1,3},{2,6},{3,1},{4,0},{5,7},{6,2},{7,5},{8,12},{9,11},{10,... | collective-permute-start | bytes 1179656 | tf_op jit(solution)/shard_map/ppermute | solution.py:590
  116.7 29.9 %copy-start.30 = (bf16[1,128,512]{2,1,0:T(8,128)(2,1)}, bf16[1,128,512]{2,1,0:T(8,128)(2,1)S(1)}, u32[]{:S(2)}) copy-start(bf16[1,128,512]{2,1,0:T(8,128)(2,1)S(1)} %collective-permute-done.12.refs_12_) | copy-start | bytes 393220
  116.8 6.4 %collective-permute-start.13 = (bf16[2,128,512]{2,1,0:T(8,128)(2,1)S(1)}, bf16[2,128,512]{2,1,0:T(8,128)(2,1)S(1)}, u32[]{:S(2)}, u32[]{:S(2)}) collective-permute-start(bf16[2,128,512]{2,1,0:T(8,128)(2,1)S(1)} %pad_maximum_fusion.3), channel_id=1, source_target_pairs={{0,2},{1,5},{2,0},{3,7},{4,6},{5,1},{6,4},{7,3},{8,10},{9,13},{10,... | collective-permute-start | bytes 786440 | tf_op jit(solution)/shard_map/ppermute | solution.py:590
  120.6 30.5 %copy-start.28 = (bf16[1,128,1536]{2,1,0:T(8,128)(2,1)}, bf16[1,128,1536]{2,1,0:T(8,128)(2,1)S(1)}, u32[]{:S(2)}) copy-start(bf16[1,128,1536]{2,1,0:T(8,128)(2,1)S(1)} %collective-permute-done.9.refs_1_) | copy-start | bytes 1179652
  124.8 27.1 %copy-start.25 = (bf16[1,128,1536]{2,1,0:T(8,128)(2,1)S(1)}, bf16[1,128,1536]{2,1,0:T(8,128)(2,1)}, u32[]{:S(2)}) copy-start(bf16[1,128,1536]{2,1,0:T(8,128)(2,1)} %copy-done.24) | copy-start | bytes 1179652
  124.9 19.8 %collective-permute-start.14 = (bf16[2,128,1536]{2,1,0:T(8,128)(2,1)}, bf16[2,128,1536]{2,1,0:T(8,128)(2,1)}, u32[]{:S(2)}, u32[]{:S(2)}) collective-permute-start(bf16[2,128,1536]{2,1,0:T(8,128)(2,1)} %after.11), channel_id=1, source_target_pairs={{0,8},{1,17},{2,10},{3,19},{4,12},{5,21},{6,14},{7,23},{8,0},{9,25... | collective-permute-start | bytes 2359304 | tf_op jit(solution)/shard_map/ppermute | solution.py:590
  125.7 26.3 %collective-permute-start.15 = (bf16[1,128,1536]{2,1,0:T(8,128)(2,1)S(1)}, bf16[1,128,1536]{2,1,0:T(8,128)(2,1)S(1)}, u32[]{:S(2)}, u32[]{:S(2)}) collective-permute-start(bf16[1,128,1536]{2,1,0:T(8,128)(2,1)S(1)} %collective-permute-done.9.refs_1_), channel_id=1, source_target_pairs={{0,4},{1,3},{2,6},{3,1},{4,0},{5,7},{6,2},{7,5},{8,12},{9,11},{10,... | collective-permute-start | bytes 1179656 | tf_op jit(solution)/shard_map/ppermute | solution.py:590
  144.7 16.7 %collective-permute-start.16 = (bf16[2,128,1536]{2,1,0:T(8,128)(2,1)}, bf16[2,128,1536]{2,1,0:T(8,128)(2,1)}, u32[]{:S(2)}, u32[]{:S(2)}) collective-permute-start(bf16[2,128,1536]{2,1,0:T(8,128)(2,1)} %collective-permute-done.14.refs_4_), channel_id=1, source_target_pairs={{0,4},{1,3},{2,6},{3,1},{4,0},{5,7},{6,2},{7,5},{8,12},{9,11},{10,... | collective-permute-start | bytes 2359304 | tf_op jit(solution)/shard_map/ppermute | solution.py:590
  148.7 16.0 %collective-permute-start.21 = (bf16[4,128,512]{2,1,0:T(8,128)(2,1)}, bf16[4,128,512]{2,1,0:T(8,128)(2,1)}, u32[]{:S(2)}, u32[]{:S(2)}) collective-permute-start(bf16[4,128,512]{2,1,0:T(8,128)(2,1)} %pad_maximum_fusion.2), channel_id=1, source_target_pairs={{0,16},{1,9},{2,18},{3,11},{4,20},{5,13},{6,22},{7,15},{8,24},{9,1... | collective-permute-start | bytes 1572872 | tf_op jit(solution)/shard_map/ppermute | solution.py:590
  151.1 11.4 %collective-permute-start.17 = (bf16[1,128,1536]{2,1,0:T(8,128)(2,1)S(1)}, bf16[1,128,1536]{2,1,0:T(8,128)(2,1)S(1)}, u32[]{:S(2)}, u32[]{:S(2)}) collective-permute-start(bf16[1,128,1536]{2,1,0:T(8,128)(2,1)S(1)} %collective-permute-done.9.refs_1_), channel_id=1, source_target_pairs={{0,2},{1,5},{2,0},{3,7},{4,6},{5,1},{6,4},{7,3},{8,10},{9,13},{10,... | collective-permute-start | bytes 1179656 | tf_op jit(solution)/shard_map/ppermute | solution.py:590
  153.0 35.2 %collective-permute-start.19 = (bf16[2,128,1536]{2,1,0:T(8,128)(2,1)}, bf16[2,128,1536]{2,1,0:T(8,128)(2,1)}, u32[]{:S(2)}, u32[]{:S(2)}) collective-permute-start(bf16[2,128,1536]{2,1,0:T(8,128)(2,1)} %pad_maximum_fusion.1), channel_id=1, source_target_pairs={{0,2},{1,5},{2,0},{3,7},{4,6},{5,1},{6,4},{7,3},{8,10},{9,13},{10,... | collective-permute-start | bytes 2359304 | tf_op jit(solution)/shard_map/ppermute | solution.py:590
  154.2 34.0 %collective-permute-start.18 = (bf16[2,128,1536]{2,1,0:T(8,128)(2,1)}, bf16[2,128,1536]{2,1,0:T(8,128)(2,1)}, u32[]{:S(2)}, u32[]{:S(2)}) collective-permute-start(bf16[2,128,1536]{2,1,0:T(8,128)(2,1)} %collective-permute-done.14.refs_4_), channel_id=1, source_target_pairs={{0,2},{1,5},{2,0},{3,7},{4,6},{5,1},{6,4},{7,3},{8,10},{9,13},{10,... | collective-permute-start | bytes 2359304 | tf_op jit(solution)/shard_map/ppermute | solution.py:590
  161.4 26.8 %collective-permute-start.20 = (bf16[2,128,1536]{2,1,0:T(8,128)(2,1)}, bf16[2,128,1536]{2,1,0:T(8,128)(2,1)}, u32[]{:S(2)}, u32[]{:S(2)}) collective-permute-start(bf16[2,128,1536]{2,1,0:T(8,128)(2,1)} %collective-permute-done.16.refs_6_), channel_id=1, source_target_pairs={{0,2},{1,5},{2,0},{3,7},{4,6},{5,1},{6,4},{7,3},{8,10},{9,13},{10,... | collective-permute-start | bytes 2359304 | tf_op jit(solution)/shard_map/ppermute | solution.py:590
  162.5 14.2 %collective-permute-start.22 = (bf16[4,128,512]{2,1,0:T(8,128)(2,1)}, bf16[4,128,512]{2,1,0:T(8,128)(2,1)}, u32[]{:S(2)}, u32[]{:S(2)}) collective-permute-start(bf16[4,128,512]{2,1,0:T(8,128)(2,1)} %pad_maximum_fusion.2), channel_id=1, source_target_pairs={{0,8},{1,17},{2,10},{3,19},{4,12},{5,21},{6,14},{7,23},{8,0},{9,25... | collective-permute-start | bytes 1572872 | tf_op jit(solution)/shard_map/ppermute | solution.py:590
  164.7 23.5 %collective-permute-start.23 = (bf16[4,128,512]{2,1,0:T(8,128)(2,1)}, bf16[4,128,512]{2,1,0:T(8,128)(2,1)}, u32[]{:S(2)}, u32[]{:S(2)}) collective-permute-start(bf16[4,128,512]{2,1,0:T(8,128)(2,1)} %collective-permute-done.21.refs_14_), channel_id=1, source_target_pairs={{0,8},{1,17},{2,10},{3,19},{4,12},{5,21},{6,14},{7,23},{8,0},{9,25... | collective-permute-start | bytes 1572872 | tf_op jit(solution)/shard_map/ppermute | solution.py:590
  219.4 16.6 %collective-permute-start.24 = (bf16[8,128,512]{2,1,0:T(8,128)(2,1)S(1)}, bf16[8,128,512]{2,1,0:T(8,128)(2,1)S(1)}, u32[]{:S(2)}, u32[]{:S(2)}) collective-permute-start(bf16[8,128,512]{2,1,0:T(8,128)(2,1)S(1)} %get-tuple-element.32), channel_id=1, source_target_pairs={{0,2},{1,5},{2,0},{3,7},{4,6},{5,1},{6,4},{7,3},{8,10},{9,13},{10,... | collective-permute-start | bytes 3145736 | tf_op jit(solution)/shard_map/ppermute | solution.py:590
  224.9 25.4 %collective-permute-start.36 = (bf16[8,128,512]{2,1,0:T(8,128)(2,1)S(1)}, bf16[8,128,512]{2,1,0:T(8,128)(2,1)S(1)}, u32[]{:S(2)}, u32[]{:S(2)}) collective-permute-start(bf16[8,128,512]{2,1,0:T(8,128)(2,1)S(1)} %get-tuple-element.38), channel_id=1, source_target_pairs={{0,8},{1,17},{2,10},{3,19},{4,12},{5,21},{6,14},{7,23},{8,0},{9,25... | collective-permute-start | bytes 3145736 | tf_op jit(solution)/shard_map/ppermute | solution.py:590
  229.5 22.9 %collective-permute-start.32 = (bf16[8,128,512]{2,1,0:T(8,128)(2,1)S(1)}, bf16[8,128,512]{2,1,0:T(8,128)(2,1)S(1)}, u32[]{:S(2)}, u32[]{:S(2)}) collective-permute-start(bf16[8,128,512]{2,1,0:T(8,128)(2,1)S(1)} %get-tuple-element.36), channel_id=1, source_target_pairs={{0,2},{1,5},{2,0},{3,7},{4,6},{5,1},{6,4},{7,3},{8,10},{9,13},{10,... | collective-permute-start | bytes 3145736 | tf_op jit(solution)/shard_map/ppermute | solution.py:590
  234.6 33.6 %collective-permute-start.28 = (bf16[8,128,512]{2,1,0:T(8,128)(2,1)S(1)}, bf16[8,128,512]{2,1,0:T(8,128)(2,1)S(1)}, u32[]{:S(2)}, u32[]{:S(2)}) collective-permute-start(bf16[8,128,512]{2,1,0:T(8,128)(2,1)S(1)} %get-tuple-element.34), channel_id=1, source_target_pairs={{0,2},{1,5},{2,0},{3,7},{4,6},{5,1},{6,4},{7,3},{8,10},{9,13},{10,... | collective-permute-start | bytes 3145736 | tf_op jit(solution)/shard_map/ppermute | solution.py:590
  236.4 34.3 %collective-permute-start.25 = (bf16[4,128,512]{2,1,0:T(8,128)(2,1)S(1)}, bf16[4,128,512]{2,1,0:T(8,128)(2,1)S(1)}, u32[]{:S(2)}, u32[]{:S(2)}) collective-permute-start(bf16[4,128,512]{2,1,0:T(8,128)(2,1)S(1)} %slice.129), channel_id=1, source_target_pairs={{0,4},{1,3},{2,6},{3,1},{4,0},{5,7},{6,2},{7,5},{8,12},{9,11},{10,... | collective-permute-start | bytes 1572872 | tf_op jit(solution)/shard_map/ppermute | solution.py:590
  250.7 22.5 %collective-permute-start.37 = (bf16[4,128,512]{2,1,0:T(8,128)(2,1)S(1)}, bf16[4,128,512]{2,1,0:T(8,128)(2,1)S(1)}, u32[]{:S(2)}, u32[]{:S(2)}) collective-permute-start(bf16[4,128,512]{2,1,0:T(8,128)(2,1)S(1)} %slice.147), channel_id=1, source_target_pairs={{0,16},{1,9},{2,18},{3,11},{4,20},{5,13},{6,22},{7,15},{8,24},{9,1... | collective-permute-start | bytes 1572872 | tf_op jit(solution)/shard_map/ppermute | solution.py:590
  252.8 20.9 %collective-permute-start.33 = (bf16[4,128,512]{2,1,0:T(8,128)(2,1)S(1)}, bf16[4,128,512]{2,1,0:T(8,128)(2,1)S(1)}, u32[]{:S(2)}, u32[]{:S(2)}) collective-permute-start(bf16[4,128,512]{2,1,0:T(8,128)(2,1)S(1)} %slice.141), channel_id=1, source_target_pairs={{0,4},{1,3},{2,6},{3,1},{4,0},{5,7},{6,2},{7,5},{8,12},{9,11},{10,... | collective-permute-start | bytes 1572872 | tf_op jit(solution)/shard_map/ppermute | solution.py:590
  268.6 9.6 %collective-permute-start.29 = (bf16[4,128,512]{2,1,0:T(8,128)(2,1)S(1)}, bf16[4,128,512]{2,1,0:T(8,128)(2,1)S(1)}, u32[]{:S(2)}, u32[]{:S(2)}) collective-permute-start(bf16[4,128,512]{2,1,0:T(8,128)(2,1)S(1)} %slice.135), channel_id=1, source_target_pairs={{0,4},{1,3},{2,6},{3,1},{4,0},{5,7},{6,2},{7,5},{8,12},{9,11},{10,... | collective-permute-start | bytes 1572872 | tf_op jit(solution)/shard_map/ppermute | solution.py:590
  270.8 11.6 %collective-permute-start.26 = (bf16[2,128,512]{2,1,0:T(8,128)(2,1)S(1)}, bf16[2,128,512]{2,1,0:T(8,128)(2,1)S(1)}, u32[]{:S(2)}, u32[]{:S(2)}) collective-permute-start(bf16[2,128,512]{2,1,0:T(8,128)(2,1)S(1)} %slice.131), channel_id=1, source_target_pairs={{0,8},{1,17},{2,10},{3,19},{4,12},{5,21},{6,14},{7,23},{8,0},{9,25... | collective-permute-start | bytes 786440 | tf_op jit(solution)/shard_map/ppermute | solution.py:590
  273.3 16.5 %collective-permute-start.38 = (bf16[2,128,512]{2,1,0:T(8,128)(2,1)S(1)}, bf16[2,128,512]{2,1,0:T(8,128)(2,1)S(1)}, u32[]{:S(2)}, u32[]{:S(2)}) collective-permute-start(bf16[2,128,512]{2,1,0:T(8,128)(2,1)S(1)} %slice.149), channel_id=1, source_target_pairs={{0,2},{1,5},{2,0},{3,7},{4,6},{5,1},{6,4},{7,3},{8,10},{9,13},{10,... | collective-permute-start | bytes 786440 | tf_op jit(solution)/shard_map/ppermute | solution.py:590
  273.8 19.2 %collective-permute-start.34 = (bf16[2,128,512]{2,1,0:T(8,128)(2,1)S(1)}, bf16[2,128,512]{2,1,0:T(8,128)(2,1)S(1)}, u32[]{:S(2)}, u32[]{:S(2)}) collective-permute-start(bf16[2,128,512]{2,1,0:T(8,128)(2,1)S(1)} %slice.143), channel_id=1, source_target_pairs={{0,8},{1,17},{2,10},{3,19},{4,12},{5,21},{6,14},{7,23},{8,0},{9,25... | collective-permute-start | bytes 786440 | tf_op jit(solution)/shard_map/ppermute | solution.py:590
  278.4 18.3 %collective-permute-start.30 = (bf16[2,128,512]{2,1,0:T(8,128)(2,1)S(1)}, bf16[2,128,512]{2,1,0:T(8,128)(2,1)S(1)}, u32[]{:S(2)}, u32[]{:S(2)}) collective-permute-start(bf16[2,128,512]{2,1,0:T(8,128)(2,1)S(1)} %slice.137), channel_id=1, source_target_pairs={{0,8},{1,17},{2,10},{3,19},{4,12},{5,21},{6,14},{7,23},{8,0},{9,25... | collective-permute-start | bytes 786440 | tf_op jit(solution)/shard_map/ppermute | solution.py:590
  282.5 16.0 %collective-permute-start.27 = (bf16[1,128,512]{2,1,0:T(8,128)(2,1)S(1)}, bf16[1,128,512]{2,1,0:T(8,128)(2,1)S(1)}, u32[]{:S(2)}, u32[]{:S(2)}) collective-permute-start(bf16[1,128,512]{2,1,0:T(8,128)(2,1)S(1)} %slice.133), channel_id=1, source_target_pairs={{0,16},{1,9},{2,18},{3,11},{4,20},{5,13},{6,22},{7,15},{8,24},{9,1... | collective-permute-start | bytes 393224 | tf_op jit(solution)/shard_map/ppermute | solution.py:590
  289.9 8.7 %collective-permute-start.39 = (bf16[1,128,512]{2,1,0:T(8,128)(2,1)S(1)}, bf16[1,128,512]{2,1,0:T(8,128)(2,1)S(1)}, u32[]{:S(2)}, u32[]{:S(2)}) collective-permute-start(bf16[1,128,512]{2,1,0:T(8,128)(2,1)S(1)} %slice.151), channel_id=1, source_target_pairs={{0,4},{1,3},{2,6},{3,1},{4,0},{5,7},{6,2},{7,5},{8,12},{9,11},{10,... | collective-permute-start | bytes 393224 | tf_op jit(solution)/shard_map/ppermute | solution.py:590
  293.1 7.3 %collective-permute-start.35 = (bf16[1,128,512]{2,1,0:T(8,128)(2,1)S(1)}, bf16[1,128,512]{2,1,0:T(8,128)(2,1)S(1)}, u32[]{:S(2)}, u32[]{:S(2)}) collective-permute-start(bf16[1,128,512]{2,1,0:T(8,128)(2,1)S(1)} %slice.145), channel_id=1, source_target_pairs={{0,16},{1,9},{2,18},{3,11},{4,20},{5,13},{6,22},{7,15},{8,24},{9,1... | collective-permute-start | bytes 393224 | tf_op jit(solution)/shard_map/ppermute | solution.py:590
  296.8 7.3 %collective-permute-start.31 = (bf16[1,128,512]{2,1,0:T(8,128)(2,1)S(1)}, bf16[1,128,512]{2,1,0:T(8,128)(2,1)S(1)}, u32[]{:S(2)}, u32[]{:S(2)}) collective-permute-start(bf16[1,128,512]{2,1,0:T(8,128)(2,1)S(1)} %slice.139), channel_id=1, source_target_pairs={{0,16},{1,9},{2,18},{3,11},{4,20},{5,13},{6,22},{7,15},{8,24},{9,1... | collective-permute-start | bytes 393224 | tf_op jit(solution)/shard_map/ppermute | solution.py:590
  (34 other events, 213.1 us)
